TPU v7x, 256 devices: a whole 4x4x8 slice. The times are simulated.
256 devices in a mesh: kv: 32 (over y, z), tp: 8 (over x, core).
Axes of the slice: x: 4, y: 4, z: 8, core: 2. Of those that a mesh axis runs over, the one named last changes fastest.
Arguments:
- queries: bfloat16 [1024, 16, 8192], P('kv', None, 'tp'), may hold values from -32 to 32
- suffix_kv: bfloat16 [1024, 16, 8, 256], P('kv', None, 'tp'), may hold values from -12 to 12
- suffix_len: int32 [1024], P('kv'), may hold values from 1 to 16, 10240 in all
- sys_kv: bfloat16 [1024, 8, 256], P('kv', 'tp'), may hold values from -4 to 4
- doc_kv: bfloat16 [32, 1024, 8, 256], P('kv', None, 'tp'), may hold values from -4 to 4
- doc_home: int32 [32], replicated, may hold values from 0 to 31, each once
- doc_of: int32 [1024], P('kv'), may hold values from 0 to 31, as said below
- conv_kv: bfloat16 [512, 256, 8, 256], P('kv', None, 'tp'), may hold values from -4 to 4
- conv_of: int32 [1024], P('kv'), may hold values from 0 to 511, as said below
Outputs:
- attended: bfloat16 [1024, 16, 8192], P(('kv', 'tp'))
Inputs may be any that keep to these rules, and one draw needn't show every extreme that they name: `doc_of`: requests of one conversation name the same document. Among the 32 requests of one index of kv, no document is named more than 2 times, and in every draw some document is named exactly 2 times by the requests of every index of kv. `conv_of`: each request's conversation is one of the 16 conversations stored on its own index of kv (conversation c on index c // 16); every conversation is named by exactly two requests.
All inputs are finite; a program needn't handle non-finite values. No bound on the sum of `suffix_len` on one device may be relied on, other than what follows from the above.
Results may differ from a plain program's by a relative error of at most 0.0065.
Values may be sent and summed in bfloat16 or wider, within the bound.
A program may use at most 128 MiB of HBM per device.

v0:
```python
from functools import reduce
import math

import jax
import jax.numpy as jnp
from jax import lax
from jax.sharding import PartitionSpec as P


def settle(values):
    return lax.optimization_barrier(values.astype(jnp.bfloat16)).astype(jnp.float32)


def attend(query_rows, cache, valid):
    depth = query_rows.shape[-1]
    scale = 1.0 / math.sqrt(depth)
    scores = (
        jnp.einsum(
            "brhgd,blhd->bhgrl", query_rows, cache[..., :depth], preferred_element_type=jnp.float32
        )
        * scale
    )
    if valid is not None:
        scores = jnp.where(valid, scores, -1e30)
    top = jnp.max(scores, axis=-1, keepdims=True)
    expo = jnp.exp(scores - top)
    total = jnp.sum(expo, axis=-1)
    mixed = jnp.einsum(
        "bhgrl,blhd->brhgd",
        expo.astype(jnp.bfloat16),
        cache[..., depth:],
        preferred_element_type=jnp.float32,
    )
    total_rows = jnp.transpose(total, (0, 3, 1, 2))
    top_rows = jnp.transpose(top[..., 0], (0, 3, 1, 2))
    return (mixed / total_rows[..., None], top_rows + jnp.log(total_rows))


def combine(first, second):
    top = jnp.maximum(first[1], second[1])
    weight_a = jnp.exp(first[1] - top)
    weight_b = jnp.exp(second[1] - top)
    lower = weight_a + weight_b
    upper = weight_b[..., None] * second[0]
    return (upper / lower[..., None], top + jnp.log(lower))


def blend(parts):
    top = reduce(jnp.maximum, [part[1] for part in parts])
    weights = [jnp.exp(part[1] - top) for part in parts]
    upper = reduce(jnp.add, [weight[..., None] * part[0] for weight, part in zip(weights, parts)])
    lower = reduce(jnp.add, weights)
    return upper / lower[..., None]


def on_device(queries, suffix_kv, suffix_len, sys_kv, doc_kv, doc_home, doc_of, conv_kv, conv_of):
    req_dev, suf, width = queries.shape
    kv_heads = suffix_kv.shape[2]
    depth = suffix_kv.shape[3] // 2
    head_group = width // (kv_heads * depth)
    heads = kv_heads * head_group
    query_rows = queries.reshape(req_dev, suf, kv_heads, head_group, depth)
    holders = lax.axis_size("kv")
    capacity = 2 * max(1, req_dev // holders)
    flat = query_rows.reshape(1, req_dev * suf, kv_heads, head_group, depth)
    start_state = (
        jnp.zeros(flat.shape, jnp.float32),
        jnp.full(flat.shape[:-1], -1e30, jnp.float32),
    )
    sys_out, sys_lse = combine(
        start_state, attend(flat, lax.all_gather(sys_kv, "kv", axis=0, tiled=True)[None], None)
    )
    places = jnp.arange(holders, dtype=jnp.int32)
    holder = jnp.sum(jnp.where(doc_of[:, None] == places[None, :], doc_home[None, :], 0), axis=1)
    request_ids = jnp.arange(req_dev, dtype=jnp.int32)
    rank = jnp.sum(
        (holder[:, None] == holder[None, :]) & (request_ids[:, None] > request_ids[None, :]), axis=1
    )
    slot = holder * capacity + rank
    placing = (jnp.arange(holders * capacity, dtype=jnp.int32)[:, None] == slot[None, :]).astype(
        jnp.bfloat16
    )
    sender_result = jnp.dot(
        placing, queries.reshape(req_dev, suf * width), preferred_element_type=jnp.float32
    )
    sender_result = sender_result.astype(jnp.bfloat16).reshape(holders, capacity, suf, width)
    piece = lax.all_gather(doc_kv, "kv", axis=0, tiled=True)
    count = piece.shape[0]
    asked = sender_result
    asked = asked.reshape(count, capacity * suf, kv_heads, head_group, depth)

    def one_doc(pair):
        mixed, lse = attend(pair[0][None], pair[1][None], None)
        return (settle(mixed[0]), lse[0])

    mixed, lse = lax.map(one_doc, (asked, piece))
    mixed = mixed.reshape(count, capacity, suf, width)
    lse = lse.reshape(count, capacity, suf, heads)
    doc_mixed = jnp.take(
        mixed.reshape(holders * capacity, suf, kv_heads, head_group, depth), slot, axis=0
    )
    paper_highest_entries = jnp.take(
        lse.reshape(holders * capacity, suf, kv_heads, head_group), slot, axis=0
    )
    local_talk = conv_of % conv_kv.shape[0]
    talk_cache = jnp.take(conv_kv, local_talk, axis=0)
    talk_part = attend(query_rows, talk_cache, None)
    positions = jnp.arange(suf, dtype=jnp.int32)
    own_part = attend(query_rows, suffix_kv, positions[:, None] >= positions[None, :])
    system_part = (sys_out.reshape(query_rows.shape), sys_lse.reshape(query_rows.shape[:-1]))
    merged = blend([system_part, (doc_mixed, paper_highest_entries), talk_part, own_part])
    live = positions[None, :] < suffix_len[:, None]
    merged = jnp.where(live[:, :, None, None, None], merged, 0.0)
    merged = merged.astype(jnp.bfloat16).reshape(req_dev, suf, width)
    return lax.all_to_all(merged, "tp", split_axis=0, concat_axis=2, tiled=True)


def solution(mesh):
    placed = (
        P("kv", None, "tp"),
        P("kv", None, "tp", None),
        P("kv"),
        P("kv", "tp", None),
        P("kv", None, "tp", None),
        P(),
        P("kv"),
        P("kv", None, "tp", None),
        P("kv"),
    )
    return jax.shard_map(
        on_device,
        mesh=mesh,
        in_specs=placed,
        out_specs=P(("kv", "tp"), None, None),
        check_vma=False,
    )
```

profile of v0, /device:TPU:1, one launch (start us, length us, event | category | flops | bytes accessed | tf_op | source)
XLA Modules:
  0.0 345.9 jit_solution(17182086009295189130)
XLA Ops:
  7.3 1.8 copy.105
  10.1 2.0 convolution_convert_fusion
  12.1 4.3 %reshape_reshape.10 = bf16[32,32,1,8,128]{4,3,1,0,2:T(8,128)(2,1)} reshape(bf16[64,16384]{1,0:T(8,128)(2,1)} %convolution_convert_fusion) | data formatting | bytes 4194304 | tf_op jit(solution)/shard_map/reshape;reshape | solution.py:90
  17.1 44.8 %all_gather.6 = bf16[1024,1,256]{2,0,1:T(8,128)(2,1)S(1)} all-gather(bf16[32,1,256]{2,0,1:T(8,128)(2,1)S(1)} %copy-done.13), channel_id=1, replica_groups=mesh['kv'=32,'tp'=8] {'kv'}, dimensions={0}, use_global_device_ids=true | all-gather | bytes 540672 | tf_op jit(solution)/shard_map/all_gather | solution.py:71
  61.9 7.9 %bitcast_reduce_fusion = (f32[8,512]{1,0:T(8,128)S(1)}, f32[1024,512,8]{1,0,2:T(8,128)}) fusion(bf16[512,8,128]{2,1,0:T(8,128)(2,1)S(1)} %bitcast.362, bf16[1,1024,1,256]{3,1,2,0:T(8,128)(2,1)S(1)} %bitcast.365), kind=kOutput, calls=%fused_computation.26 | convolution fusion | flops 1082126336 | bytes 18104320 | tf_op jit(solution)/shard_map/brhgd,blhd->bhgrl/dot_general | solution.py:18
  69.8 8.5 %fusion.13 = f32[8,512]{1,0:T(8,128)S(1)} fusion(f32[1024,512,8]{1,0,2:T(8,128)} %get-tuple-element.88, f32[8,512]{1,0:T(8,128)S(1)} %get-tuple-element.87), kind=kLoop, calls=%fused_computation.29 | loop fusion | flops 12578816 | bytes 16809984 | tf_op jit(solution)/shard_map/reduce_sum | solution.py:27
  79.7 2.8 gather_fusion.1
  83.1 3.6 %fusion.66 = (f32[32,8,16]{2,1,0:T(8,128)S(1)}, f32[32,1,8,16,16]{3,4,2,0,1:T(8,128)S(1)}) fusion(bf16[32,16,1,256]{3,1,0,2:T(8,128)(2,1)} %bitcast.372, pred[16,16]{0,1:T(8,128)(4,1)S(1)} %iota_compare_fusion.5, bf16[32,16,1024]{2,1,0:T(8,128)(2,1)S(1)} %copy-done.2), kind=kOutput, calls=%fused_computation.128 | convolution fusion | flops 16969728 | bytes 1458432 | tf_op jit(solution)/shard_map/brhgd,blhd->bhgrl/dot_general | solution.py:18
  89.5 1.5 fusion.21
  91.0 2.2 fusion.23
  93.2 1.4 slice-done.3
  94.7 5.5 %fusion.32 = f32[1,512,1,8,128]{4,1,3,2,0:T(8,128)} fusion(f32[1024,512,8]{1,0,2:T(8,128)S(1)} %bitcast.359, f32[8,512]{1,0:T(8,128)S(1)} %get-tuple-element.87, f32[512,8]{0,1:T(8,128)S(1)} %copy-done.15, f32[512,8]{0,1:T(8,128)S(1)} %bitcast.374, f32[512,8]{0,1:T(8,128)S(1)} %copy-done.14, bf16[1,1024,1,256]{3,1,2,0:T(8,128)(2,1)S(1)} %bitcast.366), kind=kOutput, calls=%fused_computation.54 | convolution fusion | flops 1087897600 | bytes 19202048 | tf_op jit(solution)/shard_map/bhgrl,blhd->brhgd/dot_general | solution.py:28
  100.1 54.0 %all-gather.2.cloned.1.call-done = bf16[32,1024,1,256]{3,1,2,0:T(8,128)(2,1)} async-done(((bf16[1,1024,1,256]{3,1,2,0:T(8,128)(2,1)}), bf16[32,1024,1,256]{3,1,2,0:T(8,128)(2,1)}) %all-gather.2.cloned.1.call-update) | async-done | bytes 16777232 | tf_op jit(solution)/shard_map/all_gather | solution.py:87
  154.1 147.4 %while.12 = (s32[]{:T(128)}, f32[32,32,1,8,128]{4,3,1,0,2:T(8,128)}, f32[32,32,1,8]{1,0,3,2:T(8,128)S(1)}, bf16[32,1024,1,256]{3,1,2,0:T(8,128)(2,1)}, bf16[32,3...) while((s32[]{:T(128)}, f32[32,32,1,8,128]{4,3,1,0,2:T(8,128)}, ...), condition=%wide.region_7.8_spmd, body=%wide.region_4.7_spmd.sunk | while | flops 135888640 | bytes 4401281 | solution.py:96
  155.0 1.3 fusion.75
  159.6 1.3 fusion.75
  164.2 1.3 fusion.75
  168.8 1.3 fusion.75
  173.4 1.3 fusion.75
  178.0 1.3 fusion.75
  182.6 1.3 fusion.75
  187.2 1.3 fusion.75
  191.9 1.3 fusion.75
  196.5 1.3 fusion.75
  201.1 1.3 fusion.75
  205.7 1.3 fusion.75
  210.3 1.3 fusion.75
  214.9 1.3 fusion.75
  219.5 1.3 fusion.75
  224.1 1.3 fusion.75
  228.7 1.3 fusion.75
  233.3 1.3 fusion.75
  237.9 1.3 fusion.75
  242.5 1.3 fusion.75
  247.2 1.3 fusion.75
  251.8 1.3 fusion.75
  256.4 1.3 fusion.75
  261.0 1.3 fusion.75
  265.6 1.3 fusion.75
  270.2 1.3 fusion.75
  274.8 1.3 fusion.75
  279.4 1.3 fusion.75
  288.6 1.3 fusion.75
  293.2 1.3 fusion.75
  297.8 1.3 fusion.75
  301.9 4.4 %gather_fusion.2 = f32[32,16,8,128]{3,2,1,0:T(8,128)} fusion(f32[64,16,8,128]{3,2,1,0:T(8,128)} %bitcast.369, s32[1024]{0:T(1024)} %pad_clamp_fusion.1), kind=kCustom, calls=%fused_computation.2 | custom fusion | bytes 4194432 | tf_op jit(solution)/shard_map/jit(_take)/gather | solution.py:99
  308.2 7.8 %select_convert_fusion = bf16[32,16,1,8,128]{4,1,3,0,2:T(8,128)(2,1)S(1)} fusion(f32[32,128,8,16]{1,3,2,0:T(8,128)} %fusion.23, f32[32,16,8,128]{3,2,1,0:T(8,128)} %gather_fusion.2, f32[32,16,1,8,128]{4,1,0,3,2:T(8,128)} %bitcast.375, f32[32,1,8,16,16]{3,4,2,0,1:T(8,128)S(1)} %copy-done.5, f32[32,16,8]{1,2,0:T(8,128)S(1)} %get-tuple-element.79, ...), kind=kOutput, calls=%fused_computation.60 | convolution fusion | flops 23724032 | bytes 10621440 | tf_op jit(solution)/shard_map/bhgrl,blhd->brhgd/dot_general | solution.py:28
  317.6 20.4 %all_to_all.18 = bf16[32,16,1024]{2,1,0:T(8,128)(2,1)S(1)} all-to-all(bf16[32,16,1024]{2,1,0:T(8,128)(2,1)} %reshape.289), channel_id=1, replica_groups=mesh['kv'=32,'tp'=8] {'tp'}, dimensions={0} | all-to-all | bytes 2097152 | tf_op jit(solution)/shard_map/all_to_all | solution.py:115
  (304 shorter events, 117.0 us)
Async XLA Ops:
  6.5 73.2 %copy-start = (bf16[16,256,1,256]{3,1,2,0:T(8,128)(2,1)S(1)}, bf16[16,256,1,256]{3,1,2,0:T(8,128)(2,1)}, u32[]{:S(2)}) copy-start(bf16[16,256,1,256]{3,1,2,0:T(8,128)(2,1)} %param.18) | copy-start | bytes 6291460
  6.5 2.6 copy-start.19
  6.5 2.6 copy-start.20
  6.5 147.6 %all-gather.2.cloned.1.call-start = ((), (), s32[]{:S(2)}) async-start(), calls=%async_computation.1 | async-start | bytes 17301504 | tf_op jit(solution)/shard_map/all_gather | solution.py:87
  12.1 4.3 %copy-start.2 = (bf16[32,16,1024]{2,1,0:T(8,128)(2,1)S(1)}, bf16[32,16,1024]{2,1,0:T(8,128)(2,1)}, u32[]{:S(2)}) copy-start(bf16[32,16,1024]{2,1,0:T(8,128)(2,1)} %param.11) | copy-start | bytes 3145732
  16.4 0.7 copy-start.13
  61.9 7.9 %copy-start.6 = (bf16[1024,1,256]{2,0,1:T(8,128)(2,1)}, bf16[1024,1,256]{2,0,1:T(8,128)(2,1)S(1)}, u32[]{:S(2)}) copy-start(bf16[1024,1,256]{2,0,1:T(8,128)(2,1)S(1)} %all_gather.6) | copy-start | bytes 1572868
  69.8 9.9 %copy-start.21 = (s32[32]{0:T(128)S(1)}, s32[32]{0:T(128)}, u32[]{:S(2)}) copy-start(s32[32]{0:T(128)} %param.19) | copy-start | bytes 388
  78.3 4.2 %copy-start.11 = (f32[8,512]{1,0:T(8,128)}, f32[8,512]{1,0:T(8,128)S(1)}, u32[]{:S(2)}) copy-start(f32[8,512]{1,0:T(8,128)S(1)} %fusion.13) | copy-start | bytes 49156
  83.1 4.4 %copy-start.18 = (s32[32]{0:T(128)S(1)}, s32[32]{0:T(128)}, u32[]{:S(2)}) copy-start(s32[32]{0:T(128)} %param.13) | copy-start | bytes 388
  83.1 5.0 %copy-start.3 = (bf16[32,256,256]{2,1,0:T(8,128)(2,1)S(1)}, bf16[32,256,256]{2,1,0:T(8,128)(2,1)}, u32[]{:S(2)}) copy-start(bf16[32,256,256]{2,1,0:T(8,128)(2,1)} %gather_fusion.1) | copy-start | bytes 12582916
  86.8 1.9 copy-start.4
  86.8 6.4 %slice-start = ((s8[16777216]{0:T(1024)(128)(4,1)}), s8[4194304]{0:T(1024)(128)(4,1)S(1)}, s32[]{:S(2)}) async-start(s8[16777216]{0:T(1024)(128)(4,1)} %bitcast.358), calls=%async_computation.2 | async-start | bytes 8388608
  88.2 5.0 %slice-start.1 = ((s8[16777216]{0:T(1024)(128)(4,1)}), s8[4194304]{0:T(1024)(128)(4,1)S(1)}, s32[]{:S(2)}) async-start(s8[16777216]{0:T(1024)(128)(4,1)} %bitcast.358), calls=%async_computation.3 | async-start | bytes 8388608
  88.6 4.5 %slice-start.2 = ((s8[16777216]{0:T(1024)(128)(4,1)}), s8[4194304]{0:T(1024)(128)(4,1)S(1)}, s32[]{:S(2)}) async-start(s8[16777216]{0:T(1024)(128)(4,1)} %bitcast.358), calls=%async_computation.4 | async-start | bytes 8388608
  90.9 3.7 %slice-start.3 = ((s8[16777216]{0:T(1024)(128)(4,1)}), s8[4194304]{0:T(1024)(128)(4,1)S(1)}, s32[]{:S(2)}) async-start(s8[16777216]{0:T(1024)(128)(4,1)} %bitcast.358), calls=%async_computation.5 | async-start | bytes 8388608
  91.0 3.7 %copy-start.7 = (bf16[1024,1,256]{2,0,1:T(8,128)(2,1)S(1)}, bf16[1024,1,256]{2,0,1:T(8,128)(2,1)}, u32[]{:S(2)}) copy-start(bf16[1024,1,256]{2,0,1:T(8,128)(2,1)} %copy-done.6) | copy-start | bytes 1572868
  91.0 3.7 %copy-start.12 = (f32[8,512]{1,0:T(8,128)S(1)}, f32[8,512]{1,0:T(8,128)}, u32[]{:S(2)}) copy-start(f32[8,512]{1,0:T(8,128)} %copy-done.11) | copy-start | bytes 49156
  91.0 3.7 %copy-start.14 = (f32[512,8]{0,1:T(8,128)S(1)}, f32[512,8]{0,1:T(8,128)}, u32[]{:S(2)}) copy-start(f32[512,8]{0,1:T(8,128)} %get-tuple-element.83) | copy-start | bytes 49156
  91.0 3.7 %copy-start.15 = (f32[512,8]{0,1:T(8,128)S(1)}, f32[512,8]{0,1:T(8,128)}, u32[]{:S(2)}) copy-start(f32[512,8]{0,1:T(8,128)} %get-tuple-element.84) | copy-start | bytes 49156
  94.7 59.5 %copy-start.9 = (f32[32,32,1,8]{1,0,3,2:T(8,128)S(1)}, f32[32,32,1,8]{1,0,3,2:T(8,128)}, u32[]{:S(2)}) copy-start(f32[32,32,1,8]{1,0,3,2:T(8,128)} %custom-call.7) | copy-start | bytes 98308
  301.9 5.3 %copy-start.8 = (f32[32,16,1,8]{1,0,3,2:T(8,128)S(1)}, f32[32,16,1,8]{1,0,3,2:T(8,128)}, u32[]{:S(2)}) copy-start(f32[32,16,1,8]{1,0,3,2:T(8,128)} %reshape.277) | copy-start | bytes 49156
  301.9 5.3 %copy-start.16 = (pred[32]{0:T(512)(128)(4,1)S(1)}, pred[32]{0:T(512)(128)(4,1)}, u32[]{:S(2)}) copy-start(pred[32]{0:T(512)(128)(4,1)} %get-tuple-element.72) | copy-start | bytes 100
  306.3 1.6 copy-start.5
  306.3 1.6 copy-start.17
  307.1 1.1 copy-start.10
  316.4 22.7 %copy-start.1 = (bf16[16,256,1,256]{3,1,2,0:T(8,128)(2,1)S(1)}, bf16[16,256,1,256]{3,1,2,0:T(8,128)(2,1)}, u32[]{:S(2)}) copy-start(bf16[16,256,1,256]{3,1,2,0:T(8,128)(2,1)} %param.18) | copy-start | bytes 6291460
Sparse Core Ops, SparseCore 0:
  10.0 144.1 all-gather.1
where the time goes:
time: 350 us; the launch traced here: 346 us
  matrix products  114 us (33%)
  local copies, waits for them, and re-layouts  72.4 us (21%)
  blocking collectives  65.1 us (19%)
  waiting for transfers between devices  54.7 us (16%)
  other arithmetic  24.5 us (7%)
  between operations  13.7 us (4%)
    dot_general x35, matrix products, attend(): jnp.einsum('bhgrl,blhd->brhgd', expo.astype(jnp.bfloat16), cache[..., dep...  57.4 us
    dot_general x35, matrix products, attend(): jnp.einsum('brhgd,blhd->bhgrl', query_rows, cache[..., :depth], preferred...  54.6 us
    all_gather x1, waiting for transfers between devices, on_device(): piece = lax.all_gather(doc_kv, 'kv', axis=0, tiled=True)  54 us
    all_gather x1, blocking collectives, on_device(): lax.all_gather(sys_kv, 'kv', axis=0, tiled=True)[None]  44.8 us
    dynamic_slice x32, local copies, waits for them, and re-layouts, on_device(): mixed, lse = lax.map(one_doc, (asked, piece))  27.1 us
    dynamic_update_slice x64, local copies, waits for them, and re-layouts, on_device(): mixed, lse = lax.map(one_doc, (asked, piece))  24.5 us
    all_to_all x1, blocking collectives, on_device(): return lax.all_to_all(merged, 'tp', split_axis=0, concat_axis=2, tiled=True)  20.4 us
    reduce_sum x35, other arithmetic, attend(): total = jnp.sum(expo, axis=-1)  20.3 us
  transfers between devices with their start and end apart: 1, of which 1 were waited for; matrix products, arithmetic and copies ran while one was open for 13% of the time, Pallas kernels for 0%

commit v1 on v0

v1 whole, which is shorter than its diff:
```python
import functools
import math

import jax
import jax.numpy as jnp
from jax import lax
from jax.experimental import pallas as pl
from jax.experimental.pallas import tpu as pltpu
from jax.sharding import PartitionSpec as P

MESH = pl.DeviceIdType.MESH
F32 = jnp.float32
BF16 = jnp.bfloat16

NY, NZ, NT = 4, 8, 8
REQ, SUF, HEADS, DEPTH = 32, 16, 8, 128
GROUPS = REQ // 2
ROWS = 2 * SUF * HEADS
DOC, CONV, SYS_Y = 1024, 256, 128
HALF = DOC // 2
LOG2E = math.log2(math.e)
SCALE2 = LOG2E / math.sqrt(DEPTH)

SLOT_A, SLOT_B, GRP_A, GRP_B, GRP_SLOT, REQ_AT = 0, 32, 64, 80, 96, 112
PLAN = 256

STAGES = ((0, 1), (1, 2), (3, 2), (5, 2), (7, 1))
PLACE_REL = (0, 1, 7, 2, 6, 3, 5, 4)


def plan_kernel(home_ref, doc_ref, conv_ref, out_ref, count_ref):
    kv = lax.axis_index("kv")
    y, z = kv // NZ, kv % NZ
    for i in range(PLAN):
        if i < 64:
            out_ref[i] = 0
    for i in range(GROUPS):
        count_ref[i] = 0

    def step(r, carry):
        group = conv_ref[r] % GROUPS
        holder = home_ref[doc_ref[r]]
        dy = lax.rem(holder // NZ - y + NY, NY)
        rel = lax.rem(holder % NZ - z + NZ, NZ)
        place = jnp.where(rel == 0, 0, jnp.where(rel <= NZ // 2, 2 * rel - 1, 2 * (NZ - rel)))
        slot = dy * NZ + place
        seen = count_ref[group]
        count_ref[group] = seen + 1
        out_ref[SLOT_A + slot + 32 * seen] = r
        out_ref[GRP_A + group + 16 * seen] = r
        out_ref[GRP_SLOT + group] = slot
        out_ref[REQ_AT + r] = group * 2 + seen
        return carry

    lax.fori_loop(0, REQ, step, 0)


def scores(keys, rows):
    return lax.dot_general(keys, rows, (((1,), (1,)), ((), ())), preferred_element_type=F32)


def mix(values, weights):
    return lax.dot_general(values, weights, (((0,), (0,)), ((), ())), preferred_element_type=F32)


def mix_t(values_t, weights):
    return lax.dot_general(values_t, weights, (((1,), (0,)), ((), ())), preferred_element_type=F32)


def main_kernel(
    plan, lens, q_hbm, suf_hbm, sys_hbm, doc_hbm, conv_hbm, out_hbm,
    q_ref, suf_ref, conv_ref, docs, sysb, qs, qin, gq, vt, sysvt, ret_o, ret_l, d_o, d_l,
    l_acc, l_m, l_t, res, outst,
    in_sem, doc_ss, doc_rs, sys_ss, sys_rs, sysy_ss, sysy_rs, q_ss, q_rs, o_ss, o_rs, e_ss, e_rs,
    x_ss, x_rs,
):
    kv, tp = lax.axis_index("kv"), lax.axis_index("tp")
    y, z = kv // NZ, kv % NZ
    z_right = y * NZ + lax.rem(z + 1, NZ)
    z_left = y * NZ + lax.rem(z + NZ - 1, NZ)

    def y_peer(k):
        return lax.rem(y + k, NY) * NZ + z

    def t_peer(k):
        return lax.rem(tp + k, NT)

    barrier = pltpu.get_barrier_semaphore()
    peers = [(z_right, tp), (z_left, tp)]
    peers += [(y_peer(k), tp) for k in range(1, NY)]
    peers += [(kv, t_peer(k)) for k in range(1, NT)]
    loads = [
        pltpu.make_async_copy(q_hbm, q_ref, in_sem.at[0]),
        pltpu.make_async_copy(sys_hbm, sysb.at[0, pl.ds(0, 32)], in_sem.at[1]),
        pltpu.make_async_copy(doc_hbm.at[0], docs.at[0], in_sem.at[2]),
        pltpu.make_async_copy(suf_hbm, suf_ref, in_sem.at[3]),
        pltpu.make_async_copy(conv_hbm, conv_ref, in_sem.at[4]),
    ]
    for load in loads:
        load.start()
    for peer in peers:
        pl.semaphore_signal(barrier, inc=1, device_id=peer, device_id_type=MESH)
    pl.semaphore_wait(barrier, len(peers))

    def remote(src, dst, ss, rs, peer):
        return pltpu.make_async_remote_copy(
            src_ref=src, dst_ref=dst, send_sem=ss, recv_sem=rs, device_id=peer, device_id_type=MESH
        )

    def doc_copy(way, hop, part):
        rel_src = (NZ - (hop - 1)) % NZ if way == 0 else hop - 1
        rel_dst = NZ - hop if way == 0 else hop
        rows = pl.ds(part * HALF, HALF)
        src = doc_hbm.at[0, rows] if hop == 1 else docs.at[rel_src, rows]
        peer = (z_right if way == 0 else z_left, tp)
        return remote(
            src, docs.at[rel_dst, rows], doc_ss.at[way, hop - 1, part], doc_rs.at[way, hop - 1, part], peer
        )

    def sys_copy(way, hop):
        rel_src = (NZ - (hop - 1)) % NZ if way == 0 else hop - 1
        rel_dst = NZ - hop if way == 0 else hop
        rows = pl.ds(0, SYS_Y) if hop < 4 else pl.ds(way * SYS_Y // 2, SYS_Y // 2)
        peer = (z_right if way == 0 else z_left, tp)
        return remote(
            sysb.at[rel_src, rows], sysb.at[rel_dst, rows],
            sys_ss.at[way, hop - 1], sys_rs.at[way, hop - 1], peer,
        )

    def sys_y_copy(k):
        return remote(
            sys_hbm, sysb.at[0, pl.ds(32 * (NY - k), 32)], sysy_ss.at[k - 1], sysy_rs.at[k - 1],
            (y_peer(k), tp),
        )

    def q_copy(k, stage):
        first, count = STAGES[stage]
        return remote(
            qs.at[pl.ds(k * NZ + first, count)], qin.at[pl.ds((NY - k) * NZ + first, count)],
            q_ss.at[k - 1, stage], q_rs.at[k - 1, stage], (y_peer(k), tp),
        )

    def o_copy(k, stage):
        first, count = STAGES[stage]
        return remote(
            ret_o.at[pl.ds(k * NZ + first, count)], d_o.at[pl.ds((NY - k) * NZ + first, count)],
            o_ss.at[k - 1, stage], o_rs.at[k - 1, stage], (y_peer(k), tp),
        )

    def e_copy(k, stage):
        first, count = STAGES[stage]
        return remote(
            ret_l.at[pl.ds(k * NZ + first, count)], d_l.at[pl.ds((NY - k) * NZ + first, count)],
            e_ss.at[k - 1, stage], e_rs.at[k - 1, stage], (y_peer(k), tp),
        )

    sent = []

    def start(copy):
        copy.start()
        sent.append(copy)

    def doc_hop(hop, part):
        for way in range(2):
            if hop == 4 and way != part:
                continue
            doc_copy(way, hop, part).wait_recv()
            if hop < 3 or (hop == 3 and way == part):
                start(doc_copy(way, hop + 1, part))

    def sys_hop(hop):
        for way in range(2):
            sys_copy(way, hop).wait_recv()
            if hop < 4:
                start(sys_copy(way, hop + 1))

    for way in range(2):
        start(doc_copy(way, 1, 0))
    for k in (1, 3, 2):
        start(sys_y_copy(k))

    loads[0].wait()

    def tile_rows(a, b):
        parts = []
        for h in range(HEADS):
            lanes = slice(h * DEPTH, (h + 1) * DEPTH)
            parts += [a[:, lanes], b[:, lanes]]
        return jnp.concatenate(parts, axis=0)

    def fill_out(s, carry):
        qs[s] = tile_rows(q_ref[plan[SLOT_A + s]], q_ref[plan[SLOT_B + s]])
        return carry

    def fill_own(s, carry):
        qin[s] = tile_rows(q_ref[plan[SLOT_A + s]], q_ref[plan[SLOT_B + s]])
        return carry

    def fill_group(g, carry):
        gq[g] = tile_rows(q_ref[plan[GRP_A + g]], q_ref[plan[GRP_B + g]])
        return carry

    lax.fori_loop(NZ, NY * NZ, fill_out, 0)
    for stage in range(len(STAGES)):
        for k in (1, 3, 2):
            start(q_copy(k, stage))
    loads[1].wait()
    for k in range(1, NY):
        sys_y_copy(k).wait_recv()
    for way in range(2):
        start(sys_copy(way, 1))
        start(doc_copy(way, 1, 1))
    lax.fori_loop(0, NZ, fill_own, 0)
    lax.fori_loop(0, GROUPS, fill_group, 0)

    def doc_stage(stage):
        first, count = STAGES[stage]
        for j in range(first, first + count):
            vt[j - first] = docs[PLACE_REL[j], :, DEPTH:].T

        def unit(i, carry):
            k = i + i // 2 - 2 * (i // 3)

            @pl.when(i > 0)
            def _():
                pltpu.make_async_remote_copy(
                    src_ref=qs.at[pl.ds(first, count)], dst_ref=qin.at[pl.ds(k * NZ + first, count)],
                    send_sem=q_ss.at[0, stage], recv_sem=q_rs.at[NY - 1 - k, stage],
                    device_id=(y_peer(k), tp), device_id_type=MESH,
                ).wait_recv()

            for j in range(first, first + count):
                s = scores(docs[PLACE_REL[j], :, :DEPTH], qin[k * NZ + j])
                top = jnp.max(s, axis=0, keepdims=True) * SCALE2
                e = jnp.exp2(s * SCALE2 - top)
                total = jnp.sum(e, axis=0, keepdims=True)
                o = mix_t(vt[j - first], e.astype(BF16))
                ret_o[k * NZ + j] = (o / total).astype(BF16)
                ret_l[k * NZ + j] = top + jnp.log(total) * LOG2E

            return carry

        lax.fori_loop(0, NY, unit, 0)
        for k in (1, 3, 2):
            start(o_copy(k, stage))
            start(e_copy(k, stage))
        for j in range(first, first + count):
            d_o[j] = ret_o[j]
            d_l[j] = ret_l[j]

    loads[3].wait()
    loads[4].wait()
    key_at = lax.broadcasted_iota(jnp.int32, (2 * SUF, ROWS), 0)
    row_at = lax.broadcasted_iota(jnp.int32, (2 * SUF, ROWS), 1)
    readable = ((row_at // SUF) % 2 == key_at // SUF) & (key_at % SUF <= row_at % SUF)

    def conv_unit(g, carry):
        rows = gq[g]
        suf = jnp.concatenate([suf_ref[plan[GRP_A + g]], suf_ref[plan[GRP_B + g]]], axis=0)
        s1 = scores(conv_ref[g, :, :DEPTH], rows)
        s2 = jnp.where(readable, scores(suf[:, :DEPTH], rows), -1e30)
        top = SCALE2 * jnp.maximum(
            jnp.max(s1, axis=0, keepdims=True), jnp.max(s2, axis=0, keepdims=True)
        )
        e1 = jnp.exp2(s1 * SCALE2 - top)
        e2 = jnp.exp2(s2 * SCALE2 - top)
        l_m[g] = top
        l_t[g] = jnp.sum(e1, axis=0, keepdims=True) + jnp.sum(e2, axis=0, keepdims=True)
        l_acc[g] = mix(conv_ref[g, :, DEPTH:], e1.astype(BF16)) + mix(suf[:, DEPTH:], e2.astype(BF16))
        return carry

    def sys_unit(g, carry):
        keys = sysb[:, :, :DEPTH].reshape(NZ * SYS_Y, DEPTH)
        s = scores(keys, gq[g])
        top = jnp.maximum(jnp.max(s, axis=0, keepdims=True) * SCALE2, l_m[g])
        e = jnp.exp2(s * SCALE2 - top)
        keep = jnp.exp2(l_m[g] - top)
        l_m[g] = top
        l_t[g] = l_t[g] * keep + jnp.sum(e, axis=0, keepdims=True)
        l_acc[g] = l_acc[g] * keep + mix_t(sysvt[...], e.astype(BF16))
        return carry

    lax.fori_loop(0, GROUPS, conv_unit, 0)
    doc_hop(1, 0)
    loads[2].wait()
    doc_stage(0)
    sys_hop(1)
    doc_hop(1, 1)
    doc_stage(1)
    sys_hop(2)
    doc_hop(2, 0)
    doc_hop(2, 1)
    doc_stage(2)
    sys_hop(3)
    doc_hop(3, 0)
    sys_hop(4)
    for rel in range(NZ):
        sysvt[:, rel * SYS_Y : (rel + 1) * SYS_Y] = sysb[rel, :, DEPTH:].T
    lax.fori_loop(0, GROUPS // 2, sys_unit, 0)
    doc_hop(3, 1)
    lax.fori_loop(GROUPS // 2, GROUPS, sys_unit, 0)
    doc_stage(3)
    doc_hop(4, 0)
    doc_hop(4, 1)
    doc_stage(4)
    for stage in range(len(STAGES)):
        for k in range(1, NY):
            o_copy(k, stage).wait_recv()
            e_copy(k, stage).wait_recv()

    def join(g, carry):
        slot = plan[GRP_SLOT + g]
        lse = d_l[slot]
        top = jnp.maximum(lse, l_m[g])
        w_doc = jnp.exp2(lse - top)
        w_loc = jnp.exp2(l_m[g] - top)
        upper = w_doc * d_o[slot].astype(F32) + w_loc * l_acc[g]
        out = (upper / (w_doc + w_loc * l_t[g])).T.astype(BF16)
        for h in range(HEADS):
            for p in range(2):
                first = (h * 2 + p) * SUF
                res[g * 2 + p, :, h * DEPTH : (h + 1) * DEPTH] = out[first : first + SUF]
        return carry

    lax.fori_loop(0, GROUPS, join, 0)
    token = lax.broadcasted_iota(jnp.int32, (SUF, HEADS * DEPTH), 0)

    def place(r, carry):
        value = res[plan[REQ_AT + r]]
        outst[r] = jnp.where(token < lens[r], value, jnp.zeros_like(value))
        return carry

    lax.fori_loop(0, REQ, place, 0)
    share = REQ // NT
    lanes = pl.ds(pl.multiple_of(tp * HEADS * DEPTH, 128), HEADS * DEPTH)

    def x_copy(k):
        return remote(
            outst.at[pl.ds(t_peer(k) * share, share)], out_hbm.at[:, :, lanes],
            x_ss.at[k - 1], x_rs.at[k - 1], (kv, t_peer(k)),
        )

    own = pltpu.make_async_copy(
        outst.at[pl.ds(tp * share, share)], out_hbm.at[:, :, lanes], in_sem.at[0]
    )
    for k in (4, 3, 5, 2, 6, 1, 7):
        start(x_copy(k))
    own.start()
    for copy in sent:
        copy.wait_send()
    own.wait()
    for k in range(1, NT):
        x_copy(k).wait_recv()


def on_device(queries, suffix_kv, suffix_len, sys_kv, doc_kv, doc_home, doc_of, conv_kv, conv_of):
    smem = pl.BlockSpec(memory_space=pltpu.SMEM)
    hbm = pl.BlockSpec(memory_space=pl.ANY)
    plan = pl.pallas_call(
        plan_kernel,
        out_shape=jax.ShapeDtypeStruct((PLAN,), jnp.int32),
        in_specs=[smem] * 3,
        out_specs=smem,
        scratch_shapes=[pltpu.SMEM((GROUPS,), jnp.int32)],
        name="plan",
    )(doc_home, doc_of, conv_of)
    dma = pltpu.SemaphoreType.DMA
    stages = len(STAGES)
    return pl.pallas_call(
        main_kernel,
        out_shape=jax.ShapeDtypeStruct((REQ // NT, SUF, NT * HEADS * DEPTH), BF16),
        in_specs=[smem] * 2 + [hbm] * 5,
        out_specs=hbm,
        scratch_shapes=[
            pltpu.VMEM((REQ, SUF, HEADS * DEPTH), BF16),
            pltpu.VMEM((REQ, SUF, 2 * DEPTH), BF16),
            pltpu.VMEM((GROUPS, CONV, 2 * DEPTH), BF16),
            pltpu.VMEM((NZ, DOC, 2 * DEPTH), BF16),
            pltpu.VMEM((NZ, SYS_Y, 2 * DEPTH), BF16),
            pltpu.VMEM((NY * NZ, ROWS, DEPTH), BF16),
            pltpu.VMEM((NY * NZ, ROWS, DEPTH), BF16),
            pltpu.VMEM((GROUPS, ROWS, DEPTH), BF16),
            pltpu.VMEM((2, DEPTH, DOC), BF16),
            pltpu.VMEM((DEPTH, NZ * SYS_Y), BF16),
            pltpu.VMEM((NY * NZ, DEPTH, ROWS), BF16),
            pltpu.VMEM((NY * NZ, 1, ROWS), F32),
            pltpu.VMEM((NY * NZ, DEPTH, ROWS), BF16),
            pltpu.VMEM((NY * NZ, 1, ROWS), F32),
            pltpu.VMEM((GROUPS, DEPTH, ROWS), F32),
            pltpu.VMEM((GROUPS, 1, ROWS), F32),
            pltpu.VMEM((GROUPS, 1, ROWS), F32),
            pltpu.VMEM((REQ, SUF, HEADS * DEPTH), BF16),
            pltpu.VMEM((REQ, SUF, HEADS * DEPTH), BF16),
            dma((5,)),
            dma((2, 4, 2)), dma((2, 4, 2)),
            dma((2, 4)), dma((2, 4)),
            dma((3,)), dma((3,)),
            dma((3, stages)), dma((3, stages)),
            dma((3, stages)), dma((3, stages)),
            dma((3, stages)), dma((3, stages)),
            dma((7,)), dma((7,)),
        ],
        compiler_params=pltpu.CompilerParams(
            collective_id=0, has_side_effects=True, vmem_limit_bytes=56 << 20
        ),
        name="cascade",
    )(
        plan,
        suffix_len,
        queries,
        suffix_kv.reshape(REQ, SUF, 2 * DEPTH),
        sys_kv.reshape(32, 2 * DEPTH),
        doc_kv.reshape(1, DOC, 2 * DEPTH),
        conv_kv.reshape(GROUPS, CONV, 2 * DEPTH),
    )


def solution(mesh):
    placed = (
        P("kv", None, "tp"),
        P("kv", None, "tp", None),
        P("kv"),
        P("kv", "tp", None),
        P("kv", None, "tp", None),
        P(),
        P("kv"),
        P("kv", None, "tp", None),
        P("kv"),
    )
    return jax.shard_map(
        on_device,
        mesh=mesh,
        in_specs=placed,
        out_specs=P(("kv", "tp"), None, None),
        check_vma=False,
    )
```

time: 350 us -> 103 us (0.29); the launches traced: 346 us -> 103 us
  matrix products: 114 us -> 0 us
  Pallas kernels: 0 us -> 100 us
  local copies, waits for them, and re-layouts: 72.4 us -> 2.26 us
  blocking collectives: 65.1 us -> 0 us
  waiting for transfers between devices: 54.7 us -> 0 us
  other arithmetic: 24.5 us -> 0 us
  between operations: 13.7 us -> 0.02 us
    dot_general x71 -> x0, matrix products: 114 us -> none  [the longest x35 57.4 us: attend(): jnp.einsum('bhgrl,blhd->brhgd', expo.astype(jnp.bfloat16), cache[..., dep...]
    pallas_call x0 -> x2, Pallas kernels: none -> 100 us  [the longest x1 98.2 us: on_device(): pl.pallas_call(main_kernel, out_shape=jax.ShapeDtypeStruct((REQ // NT, SU...]
    all_gather x1 -> x0, waiting for transfers between devices: 54 us -> none  [on_device(): piece = lax.all_gather(doc_kv, 'kv', axis=0, tiled=True)]
    all_gather x1 -> x0, blocking collectives: 44.8 us -> none  [on_device(): lax.all_gather(sys_kv, 'kv', axis=0, tiled=True)[None]]
    dynamic_slice x32 -> x0, local copies, waits for them, and re-layouts: 27.1 us -> none  [on_device(): mixed, lse = lax.map(one_doc, (asked, piece))]
    dynamic_update_slice x64 -> x0, local copies, waits for them, and re-layouts: 24.5 us -> none  [on_device(): mixed, lse = lax.map(one_doc, (asked, piece))]
    reduce_sum x37 -> x0, other arithmetic: 20.7 us -> none  [the longest x35 20.3 us: attend(): total = jnp.sum(expo, axis=-1)]
    all_to_all x1 -> x0, blocking collectives: 20.4 us -> none  [on_device(): return lax.all_to_all(merged, 'tp', split_axis=0, concat_axis=2, tiled=True)]
  transfers between devices with their start and end apart: 1 -> 0, of which waited for: 1 -> 0; matrix products, arithmetic and copies ran while one was open for 13% -> 0% of each run, Pallas kernels for 0% -> 0%
where the time goes in v1:
time: 103 us
  Pallas kernels  100 us (97%)
  local copies, waits for them, and re-layouts  2.26 us (2%)
    pallas_call x1, Pallas kernels, on_device(): pl.pallas_call(main_kernel, out_shape=jax.ShapeDtypeStruct((REQ // NT, SU...  98.2 us
    unnamed x1, local copies, waits for them, and re-layouts  2.26 us
    pallas_call x1, Pallas kernels, on_device(): pl.pallas_call(plan_kernel, out_shape=jax.ShapeDtypeStruct((PLAN,), jnp.i...  2.22 us

profile of v1, /device:TPU:1, one launch (start us, length us, event | category | flops | bytes accessed | tf_op | source)
XLA Modules:
  0.0 102.7 jit_solution(17144261906401143365)
XLA Ops:
  0.0 2.2 %plan.1 = s32[256]{0:T(256)} custom-call(s32[32]{0:T(128)} %home_ref.1, s32[32]{0:T(128)} %doc_ref.1, s32[32]{0:T(128)} %conv_ref.1), custom_call_target="tpu_custom_call" | custom-call | tf_op jit(solution)/shard_map/plan/pallas_call | solution.py:359
  2.2 98.2 %cascade.1 = bf16[4,16,8192]{2,1,0:T(8,128)(2,1)} custom-call(s32[256]{0:T(256)} %plan.1, s32[32]{0:T(128)} %lens.1, bf16[32,16,1024]{2,1,0:T(8,128)(2,1)} %q_hbm.1, bf16[32,16,256]{2,1,0:T(8,128)(2,1)} %bitcast.6, bf16[32,256]{1,0:T(8,128)(2,1)} %bitcast.7, bf16[1,1024,256]{2,1,0:T(8,128)(2,1)} %bitcast.5, bf16[16,256,256]{2,1,0:T(8,128)(2,1)} %bitcast.4), custom_call_target="tpu_custom_call" | custom-call | tf_op jit(solution)/shard_map/cascade/pallas_call | solution.py:369
  100.4 2.3 %copy.11 = bf16[4,16,8192]{2,1,0:T(8,128)(2,1)} copy(bf16[4,16,8192]{2,1,0:T(8,128)(2,1)} %cascade.1) | data formatting | bytes 2097152

commit v2 on v1

--- a/solution.py
+++ b/solution.py
@@ -70,7 +70,7 @@
 def main_kernel(
     plan, lens, q_hbm, suf_hbm, sys_hbm, doc_hbm, conv_hbm, out_hbm,
     q_ref, suf_ref, conv_ref, docs, sysb, qs, qin, gq, vt, sysvt, ret_o, ret_l, d_o, d_l,
-    l_acc, l_m, l_t, res, outst,
+    l_acc, l_m, l_t, res, outst, s_a, s_b,
     in_sem, doc_ss, doc_rs, sys_ss, sys_rs, sysy_ss, sysy_rs, q_ss, q_rs, o_ss, o_rs, e_ss, e_rs,
     x_ss, x_rs,
 ):
@@ -213,34 +213,65 @@
     lax.fori_loop(0, NZ, fill_own, 0)
     lax.fori_loop(0, GROUPS, fill_group, 0)
 
+    def attend(n, parts, done):
+        def score(u, buf, part, top):
+            first, size, score_of, _ = part
+            s = score_of(u)
+            buf[first : first + size] = s
+            high = jnp.max(s.reshape(size // 8, 8, ROWS), axis=0)
+            return high if top is None else jnp.maximum(top, high)
+
+        def weigh(u, buf, part, top, state):
+            first, size, _, mix_of = part
+            e = jnp.exp2(buf[first : first + size] * SCALE2 - top)
+            total = jnp.sum(e.reshape(size // 8, 8, ROWS), axis=0)
+            o = mix_of(u, e.astype(BF16))
+            return (o, total) if state is None else (state[0] + o, state[1] + total)
+
+        def both(u_next, buf_next, u, buf, top):
+            high = state = None
+            for part in parts:
+                high = score(u_next, buf_next, part, high)
+                state = weigh(u, buf, part, top, state)
+            done(u, state[0], jnp.sum(state[1], axis=0, keepdims=True), top)
+            return jnp.max(high, axis=0, keepdims=True) * SCALE2
+
+        def pair(i, top):
+            top = both(2 * i + 1, s_b, 2 * i, s_a, top)
+            return both(lax.rem(2 * i + 2, n), s_a, 2 * i + 1, s_b, top)
+
+        high = None
+        for part in parts:
+            high = score(0, s_a, part, high)
+        lax.fori_loop(0, n // 2, pair, jnp.max(high, axis=0, keepdims=True) * SCALE2)
+
     def doc_stage(stage):
         first, count = STAGES[stage]
-        for j in range(first, first + count):
-            vt[j - first] = docs[PLACE_REL[j], :, DEPTH:].T
-
-        def unit(i, carry):
-            k = i + i // 2 - 2 * (i // 3)
-
-            @pl.when(i > 0)
-            def _():
-                pltpu.make_async_remote_copy(
-                    src_ref=qs.at[pl.ds(first, count)], dst_ref=qin.at[pl.ds(k * NZ + first, count)],
-                    send_sem=q_ss.at[0, stage], recv_sem=q_rs.at[NY - 1 - k, stage],
-                    device_id=(y_peer(k), tp), device_id_type=MESH,
-                ).wait_recv()
-
-            for j in range(first, first + count):
-                s = scores(docs[PLACE_REL[j], :, :DEPTH], qin[k * NZ + j])
-                top = jnp.max(s, axis=0, keepdims=True) * SCALE2
-                e = jnp.exp2(s * SCALE2 - top)
-                total = jnp.sum(e, axis=0, keepdims=True)
-                o = mix_t(vt[j - first], e.astype(BF16))
-                ret_o[k * NZ + j] = (o / total).astype(BF16)
-                ret_l[k * NZ + j] = top + jnp.log(total) * LOG2E
-
-            return carry
-
-        lax.fori_loop(0, NY, unit, 0)
+        rel = PLACE_REL[first]
+        for k in (1, 3, 2):
+            q_copy(NY - k, stage).wait_recv()
+        for j in range(count):
+            vt[j] = docs[PLACE_REL[first + j], :, DEPTH:].T
+
+        def place_of(u):
+            return (u // count) * NZ + first + u % count
+
+        def rel_of(u):
+            return rel + (u % count) * (NZ - 2 * rel)
+
+        def part(at):
+            keys = pl.ds(at, HALF)
+            return (
+                at, HALF,
+                lambda u: scores(docs[rel_of(u), keys, :DEPTH], qin[place_of(u)]),
+                lambda u, e: mix_t(vt[u % count, :, at : at + HALF], e),
+            )
+
+        def done(u, acc, total, top):
+            ret_o[place_of(u)] = (acc * (1.0 / total)).astype(BF16)
+            ret_l[place_of(u)] = top + jnp.log(total) * LOG2E
+
+        attend(NY * count, [part(0), part(HALF)], done)
         for k in (1, 3, 2):
             start(o_copy(k, stage))
             start(e_copy(k, stage))
@@ -254,33 +285,46 @@
     row_at = lax.broadcasted_iota(jnp.int32, (2 * SUF, ROWS), 1)
     readable = ((row_at // SUF) % 2 == key_at // SUF) & (key_at % SUF <= row_at % SUF)
 
-    def conv_unit(g, carry):
-        rows = gq[g]
-        suf = jnp.concatenate([suf_ref[plan[GRP_A + g]], suf_ref[plan[GRP_B + g]]], axis=0)
-        s1 = scores(conv_ref[g, :, :DEPTH], rows)
-        s2 = jnp.where(readable, scores(suf[:, :DEPTH], rows), -1e30)
-        top = SCALE2 * jnp.maximum(
-            jnp.max(s1, axis=0, keepdims=True), jnp.max(s2, axis=0, keepdims=True)
-        )
-        e1 = jnp.exp2(s1 * SCALE2 - top)
-        e2 = jnp.exp2(s2 * SCALE2 - top)
+    def own_tokens(g, lanes):
+        return jnp.concatenate(
+            [suf_ref[plan[GRP_A + g], :, lanes], suf_ref[plan[GRP_B + g], :, lanes]], axis=0
+        )
+
+    conv_parts = [
+        (
+            0, CONV,
+            lambda g: scores(conv_ref[g, :, :DEPTH], gq[g]),
+            lambda g, e: mix(conv_ref[g, :, DEPTH:], e),
+        ),
+        (
+            CONV, 2 * SUF,
+            lambda g: jnp.where(readable, scores(own_tokens(g, slice(0, DEPTH)), gq[g]), -1e30),
+            lambda g, e: mix(own_tokens(g, slice(DEPTH, 2 * DEPTH)), e),
+        ),
+    ]
+
+    def conv_done(g, acc, total, top):
         l_m[g] = top
-        l_t[g] = jnp.sum(e1, axis=0, keepdims=True) + jnp.sum(e2, axis=0, keepdims=True)
-        l_acc[g] = mix(conv_ref[g, :, DEPTH:], e1.astype(BF16)) + mix(suf[:, DEPTH:], e2.astype(BF16))
-        return carry
-
-    def sys_unit(g, carry):
-        keys = sysb[:, :, :DEPTH].reshape(NZ * SYS_Y, DEPTH)
-        s = scores(keys, gq[g])
-        top = jnp.maximum(jnp.max(s, axis=0, keepdims=True) * SCALE2, l_m[g])
-        e = jnp.exp2(s * SCALE2 - top)
-        keep = jnp.exp2(l_m[g] - top)
-        l_m[g] = top
-        l_t[g] = l_t[g] * keep + jnp.sum(e, axis=0, keepdims=True)
-        l_acc[g] = l_acc[g] * keep + mix_t(sysvt[...], e.astype(BF16))
-        return carry
-
-    lax.fori_loop(0, GROUPS, conv_unit, 0)
+        l_t[g] = total
+        l_acc[g] = acc
+
+    def sys_part(at):
+        rels = pl.ds(at // SYS_Y, HALF // SYS_Y)
+        return (
+            at, HALF,
+            lambda g: scores(sysb[rels, :, :DEPTH].reshape(HALF, DEPTH), gq[g]),
+            lambda g, e: mix_t(sysvt[:, at : at + HALF], e),
+        )
+
+    def sys_done(g, acc, total, top):
+        high = jnp.maximum(l_m[g], top)
+        w_old = jnp.exp2(l_m[g] - high)
+        w_new = jnp.exp2(top - high)
+        l_m[g] = high
+        l_t[g] = l_t[g] * w_old + total * w_new
+        l_acc[g] = l_acc[g] * w_old + acc * w_new
+
+    attend(GROUPS, conv_parts, conv_done)
     doc_hop(1, 0)
     loads[2].wait()
     doc_stage(0)
@@ -296,9 +340,8 @@
     sys_hop(4)
     for rel in range(NZ):
         sysvt[:, rel * SYS_Y : (rel + 1) * SYS_Y] = sysb[rel, :, DEPTH:].T
-    lax.fori_loop(0, GROUPS // 2, sys_unit, 0)
+    attend(GROUPS, [sys_part(0), sys_part(HALF)], sys_done)
     doc_hop(3, 1)
-    lax.fori_loop(GROUPS // 2, GROUPS, sys_unit, 0)
     doc_stage(3)
     doc_hop(4, 0)
     doc_hop(4, 1)
@@ -391,6 +434,8 @@
             pltpu.VMEM((GROUPS, 1, ROWS), F32),
             pltpu.VMEM((REQ, SUF, HEADS * DEPTH), BF16),
             pltpu.VMEM((REQ, SUF, HEADS * DEPTH), BF16),
+            pltpu.VMEM((DOC, ROWS), F32),
+            pltpu.VMEM((DOC, ROWS), F32),
             dma((5,)),
             dma((2, 4, 2)), dma((2, 4, 2)),
             dma((2, 4)), dma((2, 4)),

time: 103 us -> 92.5 us (0.90)
  Pallas kernels: 100 us -> 90 us
    pallas_call x1, Pallas kernels: 98.2 us -> 87.8 us  [on_device(): pl.pallas_call(main_kernel, out_shape=jax.ShapeDtypeStruct((REQ // NT, SU...]
where the time goes in v2:
time: 92.5 us; the launch traced here: 92.3 us
  Pallas kernels  90 us (97%)
  local copies, waits for them, and re-layouts  2.26 us (2%)
    pallas_call x1, Pallas kernels, on_device(): pl.pallas_call(main_kernel, out_shape=jax.ShapeDtypeStruct((REQ // NT, SU...  87.8 us
    unnamed x1, local copies, waits for them, and re-layouts  2.26 us
    pallas_call x1, Pallas kernels, on_device(): pl.pallas_call(plan_kernel, out_shape=jax.ShapeDtypeStruct((PLAN,), jnp.i...  2.22 us

profile of v2, /device:TPU:1, one launch (start us, length us, event | category | flops | bytes accessed | tf_op | source)
XLA Modules:
  0.0 92.3 jit_solution(10865044046223194232)
XLA Ops:
  0.0 2.2 %plan.1 = s32[256]{0:T(256)} custom-call(s32[32]{0:T(128)} %home_ref.1, s32[32]{0:T(128)} %doc_ref.1, s32[32]{0:T(128)} %conv_ref.1), custom_call_target="tpu_custom_call" | custom-call | tf_op jit(solution)/shard_map/plan/pallas_call | solution.py:402
  2.2 87.8 %cascade.1 = bf16[4,16,8192]{2,1,0:T(8,128)(2,1)} custom-call(s32[256]{0:T(256)} %plan.1, s32[32]{0:T(128)} %lens.1, bf16[32,16,1024]{2,1,0:T(8,128)(2,1)} %q_hbm.1, bf16[32,16,256]{2,1,0:T(8,128)(2,1)} %bitcast.6, bf16[32,256]{1,0:T(8,128)(2,1)} %bitcast.7, bf16[1,1024,256]{2,1,0:T(8,128)(2,1)} %bitcast.5, bf16[16,256,256]{2,1,0:T(8,128)(2,1)} %bitcast.4), custom_call_target="tpu_custom_call" | custom-call | tf_op jit(solution)/shard_map/cascade/pallas_call | solution.py:412
  90.1 2.3 %copy.11 = bf16[4,16,8192]{2,1,0:T(8,128)(2,1)} copy(bf16[4,16,8192]{2,1,0:T(8,128)(2,1)} %cascade.1) | data formatting | bytes 2097152

commit v3 on v2

--- a/solution.py
+++ b/solution.py
@@ -18,6 +18,8 @@
 ROWS = 2 * SUF * HEADS
 DOC, CONV, SYS_Y = 1024, 256, 128
 HALF = DOC // 2
+PARTS = 4
+PIECE = DOC // PARTS
 LOG2E = math.log2(math.e)
 SCALE2 = LOG2E / math.sqrt(DEPTH)
 
@@ -26,22 +28,22 @@
 
 STAGES = ((0, 1), (1, 2), (3, 2), (5, 2), (7, 1))
 PLACE_REL = (0, 1, 7, 2, 6, 3, 5, 4)
+REL_PLACE = (0, 1, 3, 5, 7, 6, 4, 2)
+SYS_FIRST = 5 * SYS_Y
 
 
 def plan_kernel(home_ref, doc_ref, conv_ref, out_ref, count_ref):
     kv = lax.axis_index("kv")
     y, z = kv // NZ, kv % NZ
-    for i in range(PLAN):
-        if i < 64:
-            out_ref[i] = 0
+    for i in range(64):
+        out_ref[i] = 0
     for i in range(GROUPS):
         count_ref[i] = 0
-
-    def step(r, carry):
-        group = conv_ref[r] % GROUPS
+    for r in range(REQ):
+        group = conv_ref[r] & (GROUPS - 1)
         holder = home_ref[doc_ref[r]]
-        dy = lax.rem(holder // NZ - y + NY, NY)
-        rel = lax.rem(holder % NZ - z + NZ, NZ)
+        dy = ((holder >> 3) - y) & (NY - 1)
+        rel = (holder - z) & (NZ - 1)
         place = jnp.where(rel == 0, 0, jnp.where(rel <= NZ // 2, 2 * rel - 1, 2 * (NZ - rel)))
         slot = dy * NZ + place
         seen = count_ref[group]
@@ -50,9 +52,6 @@
         out_ref[GRP_A + group + 16 * seen] = r
         out_ref[GRP_SLOT + group] = slot
         out_ref[REQ_AT + r] = group * 2 + seen
-        return carry
-
-    lax.fori_loop(0, REQ, step, 0)
 
 
 def scores(keys, rows):
@@ -70,7 +69,7 @@
 def main_kernel(
     plan, lens, q_hbm, suf_hbm, sys_hbm, doc_hbm, conv_hbm, out_hbm,
     q_ref, suf_ref, conv_ref, docs, sysb, qs, qin, gq, vt, sysvt, ret_o, ret_l, d_o, d_l,
-    l_acc, l_m, l_t, res, outst, s_a, s_b,
+    l_acc, l_m, l_t, res, outst, s_a, s_b, p_acc, p_m, p_t,
     in_sem, doc_ss, doc_rs, sys_ss, sys_rs, sysy_ss, sysy_rs, q_ss, q_rs, o_ss, o_rs, e_ss, e_rs,
     x_ss, x_rs,
 ):
@@ -91,7 +90,7 @@
     peers += [(kv, t_peer(k)) for k in range(1, NT)]
     loads = [
         pltpu.make_async_copy(q_hbm, q_ref, in_sem.at[0]),
-        pltpu.make_async_copy(sys_hbm, sysb.at[0, pl.ds(0, 32)], in_sem.at[1]),
+        pltpu.make_async_copy(sys_hbm, sysb.at[pl.ds(0, 32)], in_sem.at[1]),
         pltpu.make_async_copy(doc_hbm.at[0], docs.at[0], in_sem.at[2]),
         pltpu.make_async_copy(suf_hbm, suf_ref, in_sem.at[3]),
         pltpu.make_async_copy(conv_hbm, conv_ref, in_sem.at[4]),
@@ -110,7 +109,7 @@
     def doc_copy(way, hop, part):
         rel_src = (NZ - (hop - 1)) % NZ if way == 0 else hop - 1
         rel_dst = NZ - hop if way == 0 else hop
-        rows = pl.ds(part * HALF, HALF)
+        rows = pl.ds(part * PIECE, PIECE)
         src = doc_hbm.at[0, rows] if hop == 1 else docs.at[rel_src, rows]
         peer = (z_right if way == 0 else z_left, tp)
         return remote(
@@ -120,16 +119,17 @@
     def sys_copy(way, hop):
         rel_src = (NZ - (hop - 1)) % NZ if way == 0 else hop - 1
         rel_dst = NZ - hop if way == 0 else hop
-        rows = pl.ds(0, SYS_Y) if hop < 4 else pl.ds(way * SYS_Y // 2, SYS_Y // 2)
+        at, size = (0, SYS_Y) if hop < 4 else (way * SYS_Y // 2, SYS_Y // 2)
         peer = (z_right if way == 0 else z_left, tp)
         return remote(
-            sysb.at[rel_src, rows], sysb.at[rel_dst, rows],
+            sysb.at[pl.ds(REL_PLACE[rel_src] * SYS_Y + at, size)],
+            sysb.at[pl.ds(REL_PLACE[rel_dst] * SYS_Y + at, size)],
             sys_ss.at[way, hop - 1], sys_rs.at[way, hop - 1], peer,
         )
 
     def sys_y_copy(k):
         return remote(
-            sys_hbm, sysb.at[0, pl.ds(32 * (NY - k), 32)], sysy_ss.at[k - 1], sysy_rs.at[k - 1],
+            sys_hbm, sysb.at[pl.ds(32 * (NY - k), 32)], sysy_ss.at[k - 1], sysy_rs.at[k - 1],
             (y_peer(k), tp),
         )
 
@@ -162,17 +162,19 @@
 
     def doc_hop(hop, part):
         for way in range(2):
-            if hop == 4 and way != part:
+            if hop == 4 and way != part // 2:
                 continue
             doc_copy(way, hop, part).wait_recv()
-            if hop < 3 or (hop == 3 and way == part):
+            if hop < 3 or (hop == 3 and way == part // 2):
                 start(doc_copy(way, hop + 1, part))
 
-    def sys_hop(hop):
+    def sys_take(hop):
         for way in range(2):
             sys_copy(way, hop).wait_recv()
-            if hop < 4:
-                start(sys_copy(way, hop + 1))
+
+    def sys_pass(hop):
+        for way in range(2):
+            start(sys_copy(way, hop + 1))
 
     for way in range(2):
         start(doc_copy(way, 1, 0))
@@ -188,10 +190,6 @@
             parts += [a[:, lanes], b[:, lanes]]
         return jnp.concatenate(parts, axis=0)
 
-    def fill_out(s, carry):
-        qs[s] = tile_rows(q_ref[plan[SLOT_A + s]], q_ref[plan[SLOT_B + s]])
-        return carry
-
     def fill_own(s, carry):
         qin[s] = tile_rows(q_ref[plan[SLOT_A + s]], q_ref[plan[SLOT_B + s]])
         return carry
@@ -200,8 +198,14 @@
         gq[g] = tile_rows(q_ref[plan[GRP_A + g]], q_ref[plan[GRP_B + g]])
         return carry
 
-    lax.fori_loop(NZ, NY * NZ, fill_out, 0)
-    for stage in range(len(STAGES)):
+    for stage, (first, count) in enumerate(STAGES):
+
+        def fill_out(i, carry, first=first, count=count):
+            s = (1 + i // count) * NZ + first + i % count
+            qs[s] = tile_rows(q_ref[plan[SLOT_A + s]], q_ref[plan[SLOT_B + s]])
+            return carry
+
+        lax.fori_loop(0, (NY - 1) * count, fill_out, 0)
         for k in (1, 3, 2):
             start(q_copy(k, stage))
     loads[1].wait()
@@ -209,7 +213,9 @@
         sys_y_copy(k).wait_recv()
     for way in range(2):
         start(sys_copy(way, 1))
-        start(doc_copy(way, 1, 1))
+    for part in range(1, PARTS):
+        for way in range(2):
+            start(doc_copy(way, 1, part))
     lax.fori_loop(0, NZ, fill_own, 0)
     lax.fori_loop(0, GROUPS, fill_group, 0)
 
@@ -272,12 +278,51 @@
             ret_l[place_of(u)] = top + jnp.log(total) * LOG2E
 
         attend(NY * count, [part(0), part(HALF)], done)
+        send_back(stage)
+
+    def send_back(stage):
+        first, count = STAGES[stage]
         for k in (1, 3, 2):
             start(o_copy(k, stage))
             start(e_copy(k, stage))
         for j in range(first, first + count):
             d_o[j] = ret_o[j]
             d_l[j] = ret_l[j]
+
+    def last_stage():
+        stage = len(STAGES) - 1
+        first, rel = STAGES[stage][0], PLACE_REL[STAGES[stage][0]]
+        for k in (1, 3, 2):
+            q_copy(NY - k, stage).wait_recv()
+
+        def part(at):
+            keys = pl.ds(at, PIECE)
+            return (
+                at, PIECE,
+                lambda u: scores(docs[rel, keys, :DEPTH], qin[u * NZ + first]),
+                lambda u, e: mix_t(vt[0, :, at : at + PIECE], e),
+            )
+
+        def hold(u, acc, total, top):
+            p_m[u] = top
+            p_t[u] = total
+            p_acc[u] = acc
+
+        def done(u, acc, total, top):
+            high = jnp.maximum(p_m[u], top)
+            w_old = jnp.exp2(p_m[u] - high)
+            w_new = jnp.exp2(top - high)
+            total = p_t[u] * w_old + total * w_new
+            ret_o[u * NZ + first] = ((p_acc[u] * w_old + acc * w_new) * (1.0 / total)).astype(BF16)
+            ret_l[u * NZ + first] = high + jnp.log(total) * LOG2E
+
+        for pieces, finish in (((0, 2), hold), ((1, 3), done)):
+            for piece in pieces:
+                at = piece * PIECE
+                doc_hop(4, piece)
+                vt[0, :, at : at + PIECE] = docs[rel, at : at + PIECE, DEPTH:].T
+            attend(NY, [part(piece * PIECE) for piece in pieces], finish)
+        send_back(stage)
 
     loads[3].wait()
     loads[4].wait()
@@ -308,13 +353,18 @@
         l_t[g] = total
         l_acc[g] = acc
 
-    def sys_part(at):
-        rels = pl.ds(at // SYS_Y, HALF // SYS_Y)
+    def sys_part(at, size):
+        keys = pl.ds(at, size)
         return (
-            at, HALF,
-            lambda g: scores(sysb[rels, :, :DEPTH].reshape(HALF, DEPTH), gq[g]),
-            lambda g, e: mix_t(sysvt[:, at : at + HALF], e),
-        )
+            at, size,
+            lambda g: scores(sysb[keys, :DEPTH], gq[g]),
+            lambda g, e: mix_t(sysvt[:, at : at + size], e),
+        )
+
+    def turn_sys(first, last):
+        for place in range(first, last):
+            at = place * SYS_Y
+            sysvt[:, at : at + SYS_Y] = sysb[at : at + SYS_Y, DEPTH:].T
 
     def sys_done(g, acc, total, top):
         high = jnp.maximum(l_m[g], top)
@@ -325,27 +375,33 @@
         l_acc[g] = l_acc[g] * w_old + acc * w_new
 
     attend(GROUPS, conv_parts, conv_done)
+    sys_take(1)
+    sys_pass(1)
     doc_hop(1, 0)
     loads[2].wait()
     doc_stage(0)
-    sys_hop(1)
     doc_hop(1, 1)
+    doc_hop(1, 2)
+    doc_hop(1, 3)
     doc_stage(1)
-    sys_hop(2)
+    sys_take(2)
     doc_hop(2, 0)
+    turn_sys(0, 5)
+    attend(GROUPS, [sys_part(0, 384), sys_part(384, SYS_FIRST - 384)], sys_done)
     doc_hop(2, 1)
+    doc_hop(2, 2)
+    doc_hop(2, 3)
+    sys_pass(2)
     doc_stage(2)
-    sys_hop(3)
-    doc_hop(3, 0)
-    sys_hop(4)
-    for rel in range(NZ):
-        sysvt[:, rel * SYS_Y : (rel + 1) * SYS_Y] = sysb[rel, :, DEPTH:].T
-    attend(GROUPS, [sys_part(0), sys_part(HALF)], sys_done)
-    doc_hop(3, 1)
+    for part in range(PARTS):
+        doc_hop(3, part)
+    sys_take(3)
+    sys_pass(3)
     doc_stage(3)
-    doc_hop(4, 0)
-    doc_hop(4, 1)
-    doc_stage(4)
+    last_stage()
+    sys_take(4)
+    turn_sys(5, 8)
+    attend(GROUPS, [sys_part(SYS_FIRST, NZ * SYS_Y - SYS_FIRST)], sys_done)
     for stage in range(len(STAGES)):
         for k in range(1, NY):
             o_copy(k, stage).wait_recv()
@@ -368,12 +424,6 @@
     lax.fori_loop(0, GROUPS, join, 0)
     token = lax.broadcasted_iota(jnp.int32, (SUF, HEADS * DEPTH), 0)
 
-    def place(r, carry):
-        value = res[plan[REQ_AT + r]]
-        outst[r] = jnp.where(token < lens[r], value, jnp.zeros_like(value))
-        return carry
-
-    lax.fori_loop(0, REQ, place, 0)
     share = REQ // NT
     lanes = pl.ds(pl.multiple_of(tp * HEADS * DEPTH, 128), HEADS * DEPTH)
 
@@ -386,9 +436,15 @@
     own = pltpu.make_async_copy(
         outst.at[pl.ds(tp * share, share)], out_hbm.at[:, :, lanes], in_sem.at[0]
     )
-    for k in (4, 3, 5, 2, 6, 1, 7):
-        start(x_copy(k))
-    own.start()
+    for k in (4, 3, 5, 2, 6, 1, 7, 0):
+        for i in range(share):
+            r = t_peer(k) * share + i
+            value = res[plan[REQ_AT + r]]
+            outst[r] = jnp.where(token < lens[r], value, jnp.zeros_like(value))
+        if k:
+            start(x_copy(k))
+        else:
+            own.start()
     for copy in sent:
         copy.wait_send()
     own.wait()
@@ -419,7 +475,7 @@
             pltpu.VMEM((REQ, SUF, 2 * DEPTH), BF16),
             pltpu.VMEM((GROUPS, CONV, 2 * DEPTH), BF16),
             pltpu.VMEM((NZ, DOC, 2 * DEPTH), BF16),
-            pltpu.VMEM((NZ, SYS_Y, 2 * DEPTH), BF16),
+            pltpu.VMEM((NZ * SYS_Y, 2 * DEPTH), BF16),
             pltpu.VMEM((NY * NZ, ROWS, DEPTH), BF16),
             pltpu.VMEM((NY * NZ, ROWS, DEPTH), BF16),
             pltpu.VMEM((GROUPS, ROWS, DEPTH), BF16),
@@ -436,8 +492,11 @@
             pltpu.VMEM((REQ, SUF, HEADS * DEPTH), BF16),
             pltpu.VMEM((DOC, ROWS), F32),
             pltpu.VMEM((DOC, ROWS), F32),
+            pltpu.VMEM((NY, DEPTH, ROWS), F32),
+            pltpu.VMEM((NY, 1, ROWS), F32),
+            pltpu.VMEM((NY, 1, ROWS), F32),
             dma((5,)),
-            dma((2, 4, 2)), dma((2, 4, 2)),
+            dma((2, 4, PARTS)), dma((2, 4, PARTS)),
             dma((2, 4)), dma((2, 4)),
             dma((3,)), dma((3,)),
             dma((3, stages)), dma((3, stages)),

time: 92.5 us -> 83.1 us (0.90)
  Pallas kernels: 90 us -> 80.7 us
    pallas_call x1, Pallas kernels: 87.8 us -> 79.1 us  [on_device(): pl.pallas_call(main_kernel, out_shape=jax.ShapeDtypeStruct((REQ // NT, SU...]
where the time goes in v3:
time: 83.1 us; the launch traced here: 83 us
  Pallas kernels  80.7 us (97%)
  local copies, waits for them, and re-layouts  2.26 us (3%)
    pallas_call x1, Pallas kernels, on_device(): pl.pallas_call(main_kernel, out_shape=jax.ShapeDtypeStruct((REQ // NT, SU...  79.1 us
    unnamed x1, local copies, waits for them, and re-layouts  2.26 us

profile of v3, /device:TPU:1, one launch (start us, length us, event | category | flops | bytes accessed | tf_op | source)
XLA Modules:
  0.0 83.0 jit_solution(2851301990601648792)
XLA Ops:
  0.0 1.6 %plan.1 = s32[256]{0:T(256)} custom-call(s32[32]{0:T(128)} %home_ref.1, s32[32]{0:T(128)} %doc_ref.1, s32[32]{0:T(128)} %conv_ref.1), custom_call_target="tpu_custom_call" | custom-call | tf_op jit(solution)/shard_map/plan/pallas_call | solution.py:458
  1.6 79.1 %cascade.1 = bf16[4,16,8192]{2,1,0:T(8,128)(2,1)} custom-call(s32[256]{0:T(256)} %plan.1, s32[32]{0:T(128)} %lens.1, bf16[32,16,1024]{2,1,0:T(8,128)(2,1)} %q_hbm.1, bf16[32,16,256]{2,1,0:T(8,128)(2,1)} %bitcast.6, bf16[32,256]{1,0:T(8,128)(2,1)} %bitcast.7, bf16[1,1024,256]{2,1,0:T(8,128)(2,1)} %bitcast.5, bf16[16,256,256]{2,1,0:T(8,128)(2,1)} %bitcast.4), custom_call_target="tpu_custom_call" | custom-call | tf_op jit(solution)/shard_map/cascade/pallas_call | solution.py:468
  80.7 2.3 %copy.11 = bf16[4,16,8192]{2,1,0:T(8,128)(2,1)} copy(bf16[4,16,8192]{2,1,0:T(8,128)(2,1)} %cascade.1) | data formatting | bytes 2097152

commit v4 on v3

--- a/solution.py
+++ b/solution.py
@@ -260,7 +260,7 @@
             vt[j] = docs[PLACE_REL[first + j], :, DEPTH:].T
 
         def place_of(u):
-            return (u // count) * NZ + first + u % count
+            return source_of(u // count) * NZ + first + u % count
 
         def rel_of(u):
             return rel + (u % count) * (NZ - 2 * rel)
@@ -276,15 +276,28 @@
         def done(u, acc, total, top):
             ret_o[place_of(u)] = (acc * (1.0 / total)).astype(BF16)
             ret_l[place_of(u)] = top + jnp.log(total) * LOG2E
+            send_back(u, stage)
 
         attend(NY * count, [part(0), part(HALF)], done)
-        send_back(stage)
-
-    def send_back(stage):
+        keep_own(stage)
+
+    def source_of(i):
+        return lax.rem(i + 1, NY)
+
+    def send_back(u, stage):
+        count = STAGES[stage][1]
+        k = source_of(u // count)
+
+        @pl.when((u % count == count - 1) & (k > 0))
+        def _():
+            o_copy(k, stage).start()
+            e_copy(k, stage).start()
+
+    def keep_own(stage):
         first, count = STAGES[stage]
-        for k in (1, 3, 2):
-            start(o_copy(k, stage))
-            start(e_copy(k, stage))
+        for k in range(1, NY):
+            sent.append(o_copy(k, stage))
+            sent.append(e_copy(k, stage))
         for j in range(first, first + count):
             d_o[j] = ret_o[j]
             d_l[j] = ret_l[j]
@@ -299,7 +312,7 @@
             keys = pl.ds(at, PIECE)
             return (
                 at, PIECE,
-                lambda u: scores(docs[rel, keys, :DEPTH], qin[u * NZ + first]),
+                lambda u: scores(docs[rel, keys, :DEPTH], qin[source_of(u) * NZ + first]),
                 lambda u, e: mix_t(vt[0, :, at : at + PIECE], e),
             )
 
@@ -313,8 +326,10 @@
             w_old = jnp.exp2(p_m[u] - high)
             w_new = jnp.exp2(top - high)
             total = p_t[u] * w_old + total * w_new
-            ret_o[u * NZ + first] = ((p_acc[u] * w_old + acc * w_new) * (1.0 / total)).astype(BF16)
-            ret_l[u * NZ + first] = high + jnp.log(total) * LOG2E
+            place = source_of(u) * NZ + first
+            ret_o[place] = ((p_acc[u] * w_old + acc * w_new) * (1.0 / total)).astype(BF16)
+            ret_l[place] = high + jnp.log(total) * LOG2E
+            send_back(u, stage)
 
         for pieces, finish in (((0, 2), hold), ((1, 3), done)):
             for piece in pieces:
@@ -322,7 +337,7 @@
                 doc_hop(4, piece)
                 vt[0, :, at : at + PIECE] = docs[rel, at : at + PIECE, DEPTH:].T
             attend(NY, [part(piece * PIECE) for piece in pieces], finish)
-        send_back(stage)
+        keep_own(stage)
 
     loads[3].wait()
     loads[4].wait()
@@ -467,9 +482,9 @@
     stages = len(STAGES)
     return pl.pallas_call(
         main_kernel,
-        out_shape=jax.ShapeDtypeStruct((REQ // NT, SUF, NT * HEADS * DEPTH), BF16),
+        out_shape=pltpu.VMEM((REQ // NT, SUF, NT * HEADS * DEPTH), BF16),
         in_specs=[smem] * 2 + [hbm] * 5,
-        out_specs=hbm,
+        out_specs=pl.BlockSpec(memory_space=pltpu.VMEM),
         scratch_shapes=[
             pltpu.VMEM((REQ, SUF, HEADS * DEPTH), BF16),
             pltpu.VMEM((REQ, SUF, 2 * DEPTH), BF16),

time: 83.1 us -> 81 us (0.975)
  local copies, waits for them, and re-layouts: 2.26 us -> 0.97 us
    unnamed x1, local copies, waits for them, and re-layouts: 2.26 us -> 0.97 us
where the time goes in v4:
time: 81 us; the launch traced here: 80.9 us
  Pallas kernels  79.9 us (99%)
  local copies, waits for them, and re-layouts  0.97 us (1%)
    pallas_call x1, Pallas kernels, on_device(): pl.pallas_call(main_kernel, out_shape=pltpu.VMEM((REQ // NT, SUF, NT * HE...  78.3 us
    pallas_call x1, Pallas kernels, on_device(): pl.pallas_call(plan_kernel, out_shape=jax.ShapeDtypeStruct((PLAN,), jnp.i...  1.63 us

profile of v4, /device:TPU:1, one launch (start us, length us, event | category | flops | bytes accessed | tf_op | source)
XLA Modules:
  0.0 80.9 jit_solution(8000286621691846976)
XLA Ops:
  0.0 1.6 %plan.1 = s32[256]{0:T(256)} custom-call(s32[32]{0:T(128)} %home_ref.1, s32[32]{0:T(128)} %doc_ref.1, s32[32]{0:T(128)} %conv_ref.1), custom_call_target="tpu_custom_call" | custom-call | tf_op jit(solution)/shard_map/plan/pallas_call | solution.py:473
  1.6 78.3 %cascade.1 = bf16[4,16,8192]{2,1,0:T(8,128)(2,1)S(1)} custom-call(s32[256]{0:T(256)} %plan.1, s32[32]{0:T(128)} %lens.1, bf16[32,16,1024]{2,1,0:T(8,128)(2,1)} %q_hbm.1, bf16[32,16,256]{2,1,0:T(8,128)(2,1)} %bitcast.6, bf16[32,256]{1,0:T(8,128)(2,1)} %bitcast.7, bf16[1,1024,256]{2,1,0:T(8,128)(2,1)} %bitcast.5, bf16[16,256,256]{2,1,0:T(8,128)(2,1)} %bitcast.4), custom_call_target="tpu_custom_call" | custom-call | tf_op jit(solution)/shard_map/cascade/pallas_call | solution.py:483
  79.9 1.0 %copy.11 = bf16[4,16,8192]{2,1,0:T(8,128)(2,1)} copy(bf16[4,16,8192]{2,1,0:T(8,128)(2,1)S(1)} %cascade.1) | data formatting | bytes 2097152

commit v5 on v4

--- a/solution.py
+++ b/solution.py
@@ -23,8 +23,7 @@
 LOG2E = math.log2(math.e)
 SCALE2 = LOG2E / math.sqrt(DEPTH)
 
-SLOT_A, SLOT_B, GRP_A, GRP_B, GRP_SLOT, REQ_AT = 0, 32, 64, 80, 96, 112
-PLAN = 256
+SLOT_A, SLOT_B, GRP_A, GRP_B, GRP_SLOT, REQ_AT = range(6)
 
 STAGES = ((0, 1), (1, 2), (3, 2), (5, 2), (7, 1))
 PLACE_REL = (0, 1, 7, 2, 6, 3, 5, 4)
@@ -32,26 +31,37 @@
 SYS_FIRST = 5 * SYS_Y
 
 
-def plan_kernel(home_ref, doc_ref, conv_ref, out_ref, count_ref):
-    kv = lax.axis_index("kv")
-    y, z = kv // NZ, kv % NZ
-    for i in range(64):
-        out_ref[i] = 0
-    for i in range(GROUPS):
-        count_ref[i] = 0
-    for r in range(REQ):
-        group = conv_ref[r] & (GROUPS - 1)
-        holder = home_ref[doc_ref[r]]
-        dy = ((holder >> 3) - y) & (NY - 1)
-        rel = (holder - z) & (NZ - 1)
-        place = jnp.where(rel == 0, 0, jnp.where(rel <= NZ // 2, 2 * rel - 1, 2 * (NZ - rel)))
-        slot = dy * NZ + place
-        seen = count_ref[group]
-        count_ref[group] = seen + 1
-        out_ref[SLOT_A + slot + 32 * seen] = r
-        out_ref[GRP_A + group + 16 * seen] = r
-        out_ref[GRP_SLOT + group] = slot
-        out_ref[REQ_AT + r] = group * 2 + seen
+def make_plan(homes, docs_of, convs, y, z):
+    shape = (REQ, 128)
+    sub = lax.broadcasted_iota(jnp.int32, shape, 0)
+    lane = lax.broadcasted_iota(jnp.int32, shape, 1)
+
+    def wide(row):
+        return jnp.concatenate([jnp.broadcast_to(row, (REQ, REQ))] * (128 // REQ), axis=1)
+
+    def column(row):
+        return jnp.sum(jnp.where(sub == lane, wide(row), 0), axis=1, keepdims=True)
+
+    doc = column(docs_of)
+    group = column(convs) & (GROUPS - 1)
+    holder = jnp.sum(jnp.where(doc == lane, wide(homes), 0), axis=1, keepdims=True)
+    dy = ((holder >> 3) - y) & (NY - 1)
+    rel = (holder - z) & (NZ - 1)
+    place = jnp.where(rel == 0, 0, jnp.where(rel <= NZ // 2, 2 * rel - 1, 2 * (NZ - rel)))
+    slot = dy * NZ + place
+    in_slot = slot == lane
+    in_group = group == lane
+    earlier = (group == (wide(convs) & (GROUPS - 1))) & (sub < lane)
+
+    def high(mask, value):
+        return jnp.max(jnp.where(mask, value, 0), axis=0, keepdims=True)
+
+    def low(mask):
+        return high(mask, REQ - sub) * -1 + REQ * high(mask, 1 + 0 * sub)
+
+    seen = high(earlier, 1 + 0 * sub)
+    own = wide(convs)[:1] & (GROUPS - 1)
+    return [low(in_slot), high(in_slot, sub), low(in_group), high(in_group, sub), high(in_group, slot), own * 2 + seen]
 
 
 def scores(keys, rows):
@@ -67,9 +77,9 @@
 
 
 def main_kernel(
-    plan, lens, q_hbm, suf_hbm, sys_hbm, doc_hbm, conv_hbm, out_hbm,
+    homes, docs_of, convs, lens, q_hbm, suf_hbm, sys_hbm, doc_hbm, conv_hbm, out_hbm,
     q_ref, suf_ref, conv_ref, docs, sysb, qs, qin, gq, vt, sysvt, ret_o, ret_l, d_o, d_l,
-    l_acc, l_m, l_t, res, outst, s_a, s_b, p_acc, p_m, p_t,
+    l_acc, l_m, l_t, res, outst, s_a, s_b, p_acc, p_m, p_t, plan_v, plan,
     in_sem, doc_ss, doc_rs, sys_ss, sys_rs, sysy_ss, sysy_rs, q_ss, q_rs, o_ss, o_rs, e_ss, e_rs,
     x_ss, x_rs,
 ):
@@ -181,7 +191,13 @@
     for k in (1, 3, 2):
         start(sys_y_copy(k))
 
+    rows = make_plan(homes[...], docs_of[...], convs[...], y, z)
+    plan_v[...] = jnp.concatenate(rows + [jnp.zeros((8 - len(rows), 128), jnp.int32)], axis=0)
+    to_scalars = pltpu.make_async_copy(plan_v, plan, in_sem.at[5])
+    to_scalars.start()
+
     loads[0].wait()
+    to_scalars.wait()
 
     def tile_rows(a, b):
         parts = []
@@ -191,18 +207,18 @@
         return jnp.concatenate(parts, axis=0)
 
     def fill_own(s, carry):
-        qin[s] = tile_rows(q_ref[plan[SLOT_A + s]], q_ref[plan[SLOT_B + s]])
+        qin[s] = tile_rows(q_ref[plan[SLOT_A, s]], q_ref[plan[SLOT_B, s]])
         return carry
 
     def fill_group(g, carry):
-        gq[g] = tile_rows(q_ref[plan[GRP_A + g]], q_ref[plan[GRP_B + g]])
+        gq[g] = tile_rows(q_ref[plan[GRP_A, g]], q_ref[plan[GRP_B, g]])
         return carry
 
     for stage, (first, count) in enumerate(STAGES):
 
         def fill_out(i, carry, first=first, count=count):
             s = (1 + i // count) * NZ + first + i % count
-            qs[s] = tile_rows(q_ref[plan[SLOT_A + s]], q_ref[plan[SLOT_B + s]])
+            qs[s] = tile_rows(q_ref[plan[SLOT_A, s]], q_ref[plan[SLOT_B, s]])
             return carry
 
         lax.fori_loop(0, (NY - 1) * count, fill_out, 0)
@@ -347,7 +363,7 @@
 
     def own_tokens(g, lanes):
         return jnp.concatenate(
-            [suf_ref[plan[GRP_A + g], :, lanes], suf_ref[plan[GRP_B + g], :, lanes]], axis=0
+            [suf_ref[plan[GRP_A, g], :, lanes], suf_ref[plan[GRP_B, g], :, lanes]], axis=0
         )
 
     conv_parts = [
@@ -423,7 +439,7 @@
             e_copy(k, stage).wait_recv()
 
     def join(g, carry):
-        slot = plan[GRP_SLOT + g]
+        slot = plan[GRP_SLOT, g]
         lse = d_l[slot]
         top = jnp.maximum(lse, l_m[g])
         w_doc = jnp.exp2(lse - top)
@@ -454,7 +470,7 @@
     for k in (4, 3, 5, 2, 6, 1, 7, 0):
         for i in range(share):
             r = t_peer(k) * share + i
-            value = res[plan[REQ_AT + r]]
+            value = res[plan[REQ_AT, r]]
             outst[r] = jnp.where(token < lens[r], value, jnp.zeros_like(value))
         if k:
             start(x_copy(k))
@@ -469,21 +485,14 @@
 
 def on_device(queries, suffix_kv, suffix_len, sys_kv, doc_kv, doc_home, doc_of, conv_kv, conv_of):
     smem = pl.BlockSpec(memory_space=pltpu.SMEM)
+    vmem = pl.BlockSpec(memory_space=pltpu.VMEM)
     hbm = pl.BlockSpec(memory_space=pl.ANY)
-    plan = pl.pallas_call(
-        plan_kernel,
-        out_shape=jax.ShapeDtypeStruct((PLAN,), jnp.int32),
-        in_specs=[smem] * 3,
-        out_specs=smem,
-        scratch_shapes=[pltpu.SMEM((GROUPS,), jnp.int32)],
-        name="plan",
-    )(doc_home, doc_of, conv_of)
     dma = pltpu.SemaphoreType.DMA
     stages = len(STAGES)
     return pl.pallas_call(
         main_kernel,
         out_shape=pltpu.VMEM((REQ // NT, SUF, NT * HEADS * DEPTH), BF16),
-        in_specs=[smem] * 2 + [hbm] * 5,
+        in_specs=[vmem] * 3 + [smem] + [hbm] * 5,
         out_specs=pl.BlockSpec(memory_space=pltpu.VMEM),
         scratch_shapes=[
             pltpu.VMEM((REQ, SUF, HEADS * DEPTH), BF16),
@@ -510,7 +519,9 @@
             pltpu.VMEM((NY, DEPTH, ROWS), F32),
             pltpu.VMEM((NY, 1, ROWS), F32),
             pltpu.VMEM((NY, 1, ROWS), F32),
-            dma((5,)),
+            pltpu.VMEM((8, 128), jnp.int32),
+            pltpu.SMEM((8, 128), jnp.int32),
+            dma((6,)),
             dma((2, 4, PARTS)), dma((2, 4, PARTS)),
             dma((2, 4)), dma((2, 4)),
             dma((3,)), dma((3,)),
@@ -524,7 +535,9 @@
         ),
         name="cascade",
     )(
-        plan,
+        doc_home.reshape(1, REQ),
+        doc_of.reshape(1, REQ),
+        conv_of.reshape(1, REQ),
         suffix_len,
         queries,
         suffix_kv.reshape(REQ, SUF, 2 * DEPTH),

time: 81 us -> 79.2 us (0.978)
  Pallas kernels: 79.9 us -> 78.1 us
    pallas_call x1 -> x0, Pallas kernels: 1.63 us -> none  [on_device(): pl.pallas_call(plan_kernel, out_shape=jax.ShapeDtypeStruct((PLAN,), jnp.i...]
where the time goes in v5:
time: 79.2 us; the launch traced here: 79.1 us
  Pallas kernels  78.1 us (99%)
  local copies, waits for them, and re-layouts  0.97 us (1%)
    pallas_call x1, Pallas kernels, on_device(): pl.pallas_call(main_kernel, out_shape=pltpu.VMEM((REQ // NT, SUF, NT * HE...  78.1 us

profile of v5, /device:TPU:1, one launch (start us, length us, event | category | flops | bytes accessed | tf_op | source)
XLA Modules:
  0.0 79.1 jit_solution(14700944991843887796)
XLA Ops:
  0.0 78.1 %cascade.1 = bf16[4,16,8192]{2,1,0:T(8,128)(2,1)S(1)} custom-call(s32[1,32]{1,0:T(1,128)} %bitcast.11, s32[1,32]{1,0:T(1,128)} %bitcast.12, s32[1,32]{1,0:T(1,128)} %bitcast.13, s32[32]{0:T(128)} %lens.1, bf16[32,16,1024]{2,1,0:T(8,128)(2,1)} %q_hbm.1, bf16[32,16,256]{2,1,0:T(8,128)(2,1)} %bitcast.9, bf16[32,256]{1,0:T(8,128)(2,1)} %bitcast.10, ...), custom_call_target="tpu_custom_call" | custom-call | tf_op jit(solution)/shard_map/cascade/pallas_call | solution.py:492
  78.1 1.0 %copy.11 = bf16[4,16,8192]{2,1,0:T(8,128)(2,1)} copy(bf16[4,16,8192]{2,1,0:T(8,128)(2,1)S(1)} %cascade.1) | data formatting | bytes 2097152

commit v6 on v5

--- a/solution.py
+++ b/solution.py
@@ -79,7 +79,7 @@
 def main_kernel(
     homes, docs_of, convs, lens, q_hbm, suf_hbm, sys_hbm, doc_hbm, conv_hbm, out_hbm,
     q_ref, suf_ref, conv_ref, docs, sysb, qs, qin, gq, vt, sysvt, ret_o, ret_l, d_o, d_l,
-    l_acc, l_m, l_t, res, outst, s_a, s_b, p_acc, p_m, p_t, plan_v, plan,
+    l_acc, l_m, l_t, outst, s_a, s_b, p_acc, p_m, p_t, plan_v, plan,
     in_sem, doc_ss, doc_rs, sys_ss, sys_rs, sysy_ss, sysy_rs, q_ss, q_rs, o_ss, o_rs, e_ss, e_rs,
     x_ss, x_rs,
 ):
@@ -201,9 +201,8 @@
 
     def tile_rows(a, b):
         parts = []
-        for h in range(HEADS):
-            lanes = slice(h * DEPTH, (h + 1) * DEPTH)
-            parts += [a[:, lanes], b[:, lanes]]
+        for rows in (a, b):
+            parts += [rows[:, h * DEPTH : (h + 1) * DEPTH] for h in range(HEADS)]
         return jnp.concatenate(parts, axis=0)
 
     def fill_own(s, carry):
@@ -359,7 +358,7 @@
     loads[4].wait()
     key_at = lax.broadcasted_iota(jnp.int32, (2 * SUF, ROWS), 0)
     row_at = lax.broadcasted_iota(jnp.int32, (2 * SUF, ROWS), 1)
-    readable = ((row_at // SUF) % 2 == key_at // SUF) & (key_at % SUF <= row_at % SUF)
+    readable = (row_at // (SUF * HEADS) == key_at // SUF) & (key_at % SUF <= row_at % SUF)
 
     def own_tokens(g, lanes):
         return jnp.concatenate(
@@ -438,22 +437,26 @@
             o_copy(k, stage).wait_recv()
             e_copy(k, stage).wait_recv()
 
-    def join(g, carry):
+    token = lax.broadcasted_iota(jnp.int32, (SUF, HEADS * DEPTH), 0)
+
+
+    def join(r):
+        at = plan[REQ_AT, r]
+        g, second = at // 2, at % 2 == 1
         slot = plan[GRP_SLOT, g]
-        lse = d_l[slot]
-        top = jnp.maximum(lse, l_m[g])
+
+        def half(rows):
+            return jnp.where(second, rows[:, ROWS // 2 :], rows[:, : ROWS // 2])
+
+        lse, local, total = half(d_l[slot]), half(l_m[g]), half(l_t[g])
+        top = jnp.maximum(lse, local)
         w_doc = jnp.exp2(lse - top)
-        w_loc = jnp.exp2(l_m[g] - top)
-        upper = w_doc * d_o[slot].astype(F32) + w_loc * l_acc[g]
-        out = (upper / (w_doc + w_loc * l_t[g])).T.astype(BF16)
-        for h in range(HEADS):
-            for p in range(2):
-                first = (h * 2 + p) * SUF
-                res[g * 2 + p, :, h * DEPTH : (h + 1) * DEPTH] = out[first : first + SUF]
-        return carry
-
-    lax.fori_loop(0, GROUPS, join, 0)
-    token = lax.broadcasted_iota(jnp.int32, (SUF, HEADS * DEPTH), 0)
+        w_loc = jnp.exp2(local - top)
+        upper = w_doc * half(d_o[slot]).astype(F32) + w_loc * half(l_acc[g])
+        out = (upper / (w_doc + w_loc * total)).T.astype(BF16)
+        rows = [out[h * SUF : (h + 1) * SUF] for h in range(HEADS)]
+        value = jnp.concatenate(rows, axis=1)
+        return jnp.where(token < lens[r], value, jnp.zeros_like(value))
 
     share = REQ // NT
     lanes = pl.ds(pl.multiple_of(tp * HEADS * DEPTH, 128), HEADS * DEPTH)
@@ -470,8 +473,7 @@
     for k in (4, 3, 5, 2, 6, 1, 7, 0):
         for i in range(share):
             r = t_peer(k) * share + i
-            value = res[plan[REQ_AT, r]]
-            outst[r] = jnp.where(token < lens[r], value, jnp.zeros_like(value))
+            outst[r] = join(r)
         if k:
             start(x_copy(k))
         else:
@@ -512,7 +514,6 @@
             pltpu.VMEM((GROUPS, DEPTH, ROWS), F32),
             pltpu.VMEM((GROUPS, 1, ROWS), F32),
             pltpu.VMEM((GROUPS, 1, ROWS), F32),
-            pltpu.VMEM((REQ, SUF, HEADS * DEPTH), BF16),
             pltpu.VMEM((REQ, SUF, HEADS * DEPTH), BF16),
             pltpu.VMEM((DOC, ROWS), F32),
             pltpu.VMEM((DOC, ROWS), F32),

time: 79.2 us -> 77.3 us (0.976)
  Pallas kernels: 78.1 us -> 76.3 us
    pallas_call x1, Pallas kernels: 78.1 us -> 76.3 us  [on_device(): pl.pallas_call(main_kernel, out_shape=pltpu.VMEM((REQ // NT, SUF, NT * HE...]
where the time goes in v6:
time: 77.3 us; the launch traced here: 77.2 us
  Pallas kernels  76.3 us (99%)
  local copies, waits for them, and re-layouts  0.97 us (1%)
    pallas_call x1, Pallas kernels, on_device(): pl.pallas_call(main_kernel, out_shape=pltpu.VMEM((REQ // NT, SUF, NT * HE...  76.3 us

profile of v6, /device:TPU:1, one launch (start us, length us, event | category | flops | bytes accessed | tf_op | source)
XLA Modules:
  0.0 77.2 jit_solution(10816964580009286759)
XLA Ops:
  0.0 76.3 %cascade.1 = bf16[4,16,8192]{2,1,0:T(8,128)(2,1)S(1)} custom-call(s32[1,32]{1,0:T(1,128)} %bitcast.11, s32[1,32]{1,0:T(1,128)} %bitcast.12, s32[1,32]{1,0:T(1,128)} %bitcast.13, s32[32]{0:T(128)} %lens.1, bf16[32,16,1024]{2,1,0:T(8,128)(2,1)} %q_hbm.1, bf16[32,16,256]{2,1,0:T(8,128)(2,1)} %bitcast.9, bf16[32,256]{1,0:T(8,128)(2,1)} %bitcast.10, ...), custom_call_target="tpu_custom_call" | custom-call | tf_op jit(solution)/shard_map/cascade/pallas_call | solution.py:494
  76.3 1.0 %copy.11 = bf16[4,16,8192]{2,1,0:T(8,128)(2,1)} copy(bf16[4,16,8192]{2,1,0:T(8,128)(2,1)S(1)} %cascade.1) | data formatting | bytes 2097152

commit v7 on v6

--- a/solution.py
+++ b/solution.py
@@ -221,7 +221,7 @@
             return carry
 
         lax.fori_loop(0, (NY - 1) * count, fill_out, 0)
-        for k in (1, 3, 2):
+        for k in (2, 1, 3):
             start(q_copy(k, stage))
     loads[1].wait()
     for k in range(1, NY):

time: 77.3 us -> 77.3 us (level)
  no operation moved by 1% of the time
where the time goes in v7:
time: 77.3 us; the launch traced here: 77.2 us
  Pallas kernels  76.2 us (99%)
  local copies, waits for them, and re-layouts  0.97 us (1%)
    pallas_call x1, Pallas kernels, on_device(): pl.pallas_call(main_kernel, out_shape=pltpu.VMEM((REQ // NT, SUF, NT * HE...  76.2 us

profile of v7, /device:TPU:1, one launch (start us, length us, event | category | flops | bytes accessed | tf_op | source)
XLA Modules:
  0.0 77.2 jit_solution(3276905493475063888)
XLA Ops:
  0.0 76.2 %cascade.1 = bf16[4,16,8192]{2,1,0:T(8,128)(2,1)S(1)} custom-call(s32[1,32]{1,0:T(1,128)} %bitcast.11, s32[1,32]{1,0:T(1,128)} %bitcast.12, s32[1,32]{1,0:T(1,128)} %bitcast.13, s32[32]{0:T(128)} %lens.1, bf16[32,16,1024]{2,1,0:T(8,128)(2,1)} %q_hbm.1, bf16[32,16,256]{2,1,0:T(8,128)(2,1)} %bitcast.9, bf16[32,256]{1,0:T(8,128)(2,1)} %bitcast.10, ...), custom_call_target="tpu_custom_call" | custom-call | tf_op jit(solution)/shard_map/cascade/pallas_call | solution.py:494
  76.2 1.0 %copy.11 = bf16[4,16,8192]{2,1,0:T(8,128)(2,1)} copy(bf16[4,16,8192]{2,1,0:T(8,128)(2,1)S(1)} %cascade.1) | data formatting | bytes 2097152
